TPU v7x, 512 devices: a whole 4x8x8 slice. The times are simulated.
512 devices in a mesh: leaf: 64 (over x, z, core), site: 8 (over y).
Axes of the slice: x: 4, y: 8, z: 8, core: 2. Of those that a mesh axis runs over, the one named last changes fastest.
Arguments:
- tips: float32 [512, 64, 1024], P('leaf', None, 'site'), as said below
- parents: int32 [896], P('leaf'), may hold values from 8 to 14, as said below
- branch_lengths: float32 [896], P('leaf'), may hold values from 0.02 to 0.6
- top_parents: int32 [126], replicated, may hold values from 64 to 126, as said below
- top_lengths: float32 [126], replicated, may hold values from 0.02 to 0.6
- weights: int32 [1024], P('site'), may hold values from 1 to 16
- eig_vectors: float32 [64, 64], replicated, as said below
- eig_inverse: float32 [64, 64], replicated, as said below
- eig_values: float32 [64], replicated, as said below
- labeled_rates: float32 [64, 64], replicated, as said below
- root_freq: float32 [64], replicated, as said below
Outputs:
- local_counts: float32 [896], P('leaf')
- top_counts: float32 [126], replicated
- site_loglik: float32 [1024], P('site')
Inputs may be any that keep to these rules, and one draw needn't show every extreme that they name: `parents`: within each block of 14 entries (one subtree) the entries form a binary tree: every entry is larger than its own position in the block, every internal node 8 to 14 is named by exactly two entries. `top_parents`: A binary tree over the subtrees: every entry is larger than its own position, every node 64 to 2 * 64 - 2 is named by exactly two entries. `tips`: Positive. eig_vectors diag(eig_values) eig_inverse is a reversible rate matrix Q on the first 61 states with stationary frequencies root_freq and mean rate 1, and eig_inverse eig_vectors is the identity; rows, columns and eigenvalues past 61 are those of the identity and 0. `eig_inverse`: the inverse of eig_vectors, as above. `eig_values`: eigenvalues of Q, at most 0. `labeled_rates`: Off-diagonal rates of Q for a symmetric set of counted state pairs, 0 elsewhere. `root_freq`: positive on the first 61 states, 0 past them, summing to 1.
All inputs are finite; a program needn't handle non-finite values.
Results may differ from a plain program's by a relative error of at most 0.0003.
Values sent between devices are 32-bit elements; how exact they have to be, the bound alone decides.
A program may use at most 64 MiB of HBM per device.

v0:
```python
import jax
import jax.numpy as jnp
from jax import lax
from jax.sharding import PartitionSpec as P

CODONS = 61


PRECISE = lax.Precision.HIGHEST


def propagate(eig_vectors, eig_inverse, eig_values, branch, partial_value):
    projected = jnp.dot(eig_inverse, partial_value, precision=PRECISE)
    damping = jnp.exp(eig_values * branch)
    return jnp.dot(eig_vectors, damping[:, None] * projected, precision=PRECISE)


def integrals(eig_values, branch):
    spread = (eig_values[:, None] - eig_values[None, :]) * branch
    near_zero = jnp.abs(spread) < 0.0001
    divisor = jnp.where(near_zero, jnp.ones_like(spread), spread)
    growth = jnp.where(
        near_zero, 1.0 + spread / 2.0 + spread * spread / 6.0, jnp.expm1(spread) / divisor
    )
    return branch * jnp.exp(eig_values[None, :] * branch) * growth


def climb_tree(leaf_rows, tree_links, lengths, eig_vectors, eig_inverse, eig_values):
    leaf_count = leaf_rows.shape[0]
    edge_count = tree_links.shape[0]
    inside = jnp.concatenate(
        [
            leaf_rows,
            jnp.ones((leaf_count - 1, leaf_rows.shape[1], leaf_rows.shape[2]), jnp.float32),
        ],
        axis=0,
    )

    def finish(inside, log_scale, position):
        node_row = lax.dynamic_index_in_dim(inside, position, 0, keepdims=False)
        biggest = jnp.max(node_row, axis=0)
        internal = position >= leaf_count
        node_row = jnp.where(internal, node_row / biggest, node_row)
        log_scale = log_scale + jnp.where(internal, jnp.log(biggest), jnp.zeros_like(biggest))
        return (lax.dynamic_update_index_in_dim(inside, node_row, position, 0), log_scale, node_row)

    def climb_visit(position, state_pair):
        inside, log_scale = state_pair
        inside, log_scale, node_row = finish(inside, log_scale, position)
        message = propagate(eig_vectors, eig_inverse, eig_values, lengths[position], node_row)
        parent_node = tree_links[position]
        target = lax.dynamic_index_in_dim(inside, parent_node, 0, keepdims=False) * message
        return (lax.dynamic_update_index_in_dim(inside, target, parent_node, 0), log_scale)

    log_scale = jnp.zeros((leaf_rows.shape[2],), jnp.float32)
    inside, log_scale = lax.fori_loop(0, edge_count, climb_visit, (inside, log_scale))
    inside, log_scale, _ = finish(inside, log_scale, edge_count)
    return (inside, log_scale)


def descend(
    inside, tree_links, lengths, root_out, weight, eig_vectors, eig_inverse, eig_values, count_basis
):
    node_count = inside.shape[0]
    edge_count = node_count - 1
    labels = jnp.arange(node_count, dtype=jnp.int32)
    edges = jnp.arange(edge_count, dtype=jnp.int32)
    member = tree_links[None, :] == labels[:, None]
    child_sum = jnp.sum(jnp.where(member, edges[None, :], 0), axis=1)
    sibling = child_sum[tree_links] - edges
    outside = jnp.zeros_like(inside).at[node_count - 1].set(root_out)

    def descend_visit(counter, state_pair):
        outside, totals = state_pair
        position = edge_count - 1 - counter
        parent_node = tree_links[position]
        beside = sibling[position]
        branch = lengths[position]
        partner = propagate(
            eig_vectors,
            eig_inverse,
            eig_values,
            lengths[beside],
            lax.dynamic_index_in_dim(inside, beside, 0, keepdims=False),
        )
        arriving = lax.dynamic_index_in_dim(outside, parent_node, 0, keepdims=False) * partner
        weighted = jnp.dot(eig_vectors.T, arriving, precision=PRECISE)
        projected = jnp.dot(
            eig_inverse,
            lax.dynamic_index_in_dim(inside, position, 0, keepdims=False),
            precision=PRECISE,
        )
        damping = jnp.exp(eig_values * branch)
        denominator = jnp.sum(weighted * damping[:, None] * projected, axis=0)
        mixed_rows = jnp.dot(
            count_basis * integrals(eig_values, branch), projected, precision=PRECISE
        )
        numerator = jnp.sum(weighted * mixed_rows, axis=0)
        pattern_total = jnp.sum(weight * numerator / denominator)
        outward = jnp.dot(eig_inverse.T, damping[:, None] * weighted, precision=PRECISE)
        outward = outward / jnp.max(outward, axis=0)
        outside = lax.dynamic_update_index_in_dim(outside, outward, position, 0)
        return (outside, totals.at[position].set(pattern_total))

    totals = jnp.zeros((edge_count,), jnp.float32)
    return lax.fori_loop(0, edge_count, descend_visit, (outside, totals))


def joining_tree(
    root_rows,
    top_parents,
    top_lengths,
    root_start,
    weight,
    eig_vectors,
    eig_inverse,
    eig_values,
    count_basis,
):
    top_inside, top_logs = climb_tree(
        root_rows, top_parents, top_lengths, eig_vectors, eig_inverse, eig_values
    )
    top_outside, top_totals = descend(
        top_inside,
        top_parents,
        top_lengths,
        root_start,
        weight,
        eig_vectors,
        eig_inverse,
        eig_values,
        count_basis,
    )
    return (top_inside[-1], top_logs, top_outside, top_totals)


def on_device(
    tips,
    parents,
    branch_lengths,
    top_parents,
    top_lengths,
    weights,
    eig_vectors,
    eig_inverse,
    eig_values,
    labeled_rates,
    root_freq,
):
    states = tips.shape[1]
    columns = tips.shape[2]
    codon_mask = (jnp.arange(states) < CODONS).astype(jnp.float32)
    count_basis = jnp.dot(
        jnp.dot(eig_inverse, labeled_rates, precision=PRECISE), eig_vectors, precision=PRECISE
    )
    inside, local_logs = climb_tree(
        tips * codon_mask[None, :, None],
        parents,
        branch_lengths,
        eig_vectors,
        eig_inverse,
        eig_values,
    )
    subtree_root = inside[-1]
    groups = lax.axis_size("leaf")
    member_index = lax.axis_index("leaf")
    taxon_count = tips.shape[0] * groups
    weight = weights.astype(jnp.float32)
    share_width = columns // groups
    root_rows, root_logs = (
        lax.all_to_all(subtree_root[None], "leaf", split_axis=2, concat_axis=0, tiled=True),
        lax.all_to_all(local_logs[None, None], "leaf", split_axis=2, concat_axis=0, tiled=True),
    )
    weight_share = lax.dynamic_slice_in_dim(weight, member_index * share_width, share_width)
    root_start = jnp.broadcast_to(root_freq[:, None], (states, share_width))
    top_root, top_logs, top_outside, top_totals = joining_tree(
        root_rows,
        top_parents,
        top_lengths,
        root_start,
        weight_share,
        eig_vectors,
        eig_inverse,
        eig_values,
        count_basis,
    )
    likelihood = jnp.sum(root_freq[:, None] * top_root, axis=0)
    part_loglik = (jnp.log(likelihood) + top_logs + jnp.sum(root_logs[:, 0], axis=0)) / taxon_count
    loglik_rows = jnp.broadcast_to(part_loglik[None, None, :], (groups, 1, share_width))
    returned, returned_loglik = (
        lax.all_to_all(top_outside[:groups], "leaf", split_axis=0, concat_axis=2, tiled=True),
        lax.all_to_all(loglik_rows, "leaf", split_axis=0, concat_axis=2, tiled=True),
    )
    site_loglik = returned_loglik[0, 0]
    _, local_totals = descend(
        inside,
        parents,
        branch_lengths,
        returned[0],
        weight,
        eig_vectors,
        eig_inverse,
        eig_values,
        count_basis,
    )
    local_sum, weight_total = lax.psum((local_totals, jnp.sum(weight)), "site")
    top_sum = lax.psum(top_totals, ("leaf", "site"))
    return (local_sum / weight_total, top_sum / weight_total, site_loglik)


def solution(mesh):
    placed = (
        P("leaf", None, "site"),
        P("leaf"),
        P("leaf"),
        P(),
        P(),
        P("site"),
        P(),
        P(),
        P(),
        P(),
        P(),
    )
    return jax.shard_map(
        on_device,
        mesh=mesh,
        in_specs=placed,
        out_specs=(P("leaf"), P(), P("site")),
        check_vma=False,
    )
```

profile of v0, /device:TPU:1, one launch (start us, length us, event | category | flops | bytes accessed | tf_op | source)
XLA Modules:
  0.0 2468.6 jit_solution(14926686396223538891)
XLA Ops:
  2.5 59.4 %while.72 = (s32[]{:T(128)}, f32[15,64,128]{2,1,0:T(8,128)S(1)}, f32[128]{0:T(128)S(1)}, s32[14]{0:T(128)S(1)}, f32[14]{0:T(128)S(1)}, /*index=5*/f32[64]{0:T(12...) while((s32[]{:T(128)}, f32[15,64,128]{2,1,0:T(8,128)S(1)}, ...), condition=%wide.region_3.4_spmd.clone, body=%wide.region_1.3_spmd.clone.sunk | while | flops 12640583 | bytes 397541 | solution.py:56
  62.6 14.8 all-to-all-start.2
  78.4 1.2 gather_fusion
  82.7 4.6 all-to-all-done.2
  87.3 5.8 all-to-all-start
  95.6 6.7 all-to-all-done
  103.7 598.3 %while.73 = (s32[]{:T(128)}, f32[127,64,2]{1,2,0:T(2,128)S(1)}, f32[2]{0:T(128)S(1)}, s32[126]{0:T(128)S(1)}, f32[126]{0:T(128)S(1)}, /*index=5*/f32[64]{0:T(128...) while((s32[]{:T(128)}, f32[127,64,2]{1,2,0:T(2,128)S(1)}, ...), condition=%wide.region_7.8_spmd.clone, body=%wide.region_5.7_spmd.clone.sunk | while | flops 197579 | bytes 76037 | solution.py:56
  702.4 1478.6 %while.70 = (s32[]{:T(128)}, f32[127,64,2]{1,2,0:T(2,128)S(1)}, f32[126]{0:T(128)S(1)}, f32[126]{0:T(128)S(1)}, f32[64]{0:T(128)S(1)}, /*index=5*/s32[126]{0:T(1...) while((s32[]{:T(128)}, f32[127,64,2]{1,2,0:T(2,128)S(1)}, ...), condition=%wide.region_14.15_spmd, body=%wide.region_9.14_spmd.sunk | while | flops 648659 | bytes 146663 | solution.py:106
  744.6 1.2 broadcast_multiply_fusion.5
  756.3 1.2 broadcast_multiply_fusion.5
  815.0 1.2 broadcast_multiply_fusion.5
  826.7 1.2 broadcast_multiply_fusion.5
  885.4 1.2 broadcast_multiply_fusion.5
  897.1 1.2 broadcast_multiply_fusion.5
  908.9 1.2 broadcast_multiply_fusion.5
  967.6 1.2 broadcast_multiply_fusion.5
  979.3 1.2 broadcast_multiply_fusion.5
  1038.0 1.2 broadcast_multiply_fusion.5
  1049.7 1.2 broadcast_multiply_fusion.5
  1108.4 1.2 broadcast_multiply_fusion.5
  1120.1 1.2 broadcast_multiply_fusion.5
  1131.9 1.2 broadcast_multiply_fusion.5
  1190.5 1.2 broadcast_multiply_fusion.5
  1202.3 1.2 broadcast_multiply_fusion.5
  1260.9 1.2 broadcast_multiply_fusion.5
  1272.7 1.2 broadcast_multiply_fusion.5
  2181.7 4.7 all-to-all-start.3
  2187.1 8.7 all-to-all-done.3
  2195.8 4.7 all-to-all-start.1
  2201.1 99.4 %psum.23 = f32[126]{0:T(128)S(1)} all-reduce(f32[126]{0:T(128)S(1)} %get-tuple-element.930), channel_id=1, replica_groups=mesh['leaf'=64,'site'=8] {'leaf','site'}, use_global_device_ids=true, to_apply=%region_25.26 | all-reduce | flops 126 | bytes 1008 | tf_op jit(solution)/shard_map/psum | solution.py:207
  2303.3 150.2 %while.71 = (s32[]{:T(128)}, f32[15,64,128]{2,1,0:T(8,128)S(1)}, f32[14]{0:T(128)S(1)}, f32[14]{0:T(128)S(1)}, f32[64]{0:T(128)S(1)}, /*index=5*/s32[14]{0:T(128...) while((s32[]{:T(128)}, f32[15,64,128]{2,1,0:T(8,128)S(1)}, ...), condition=%wide.region_21.22_spmd, body=%wide.region_16.21_spmd.sunk | while | flops 37888208 | bytes 662327 | solution.py:106
  2453.5 12.7 all-reduce.4
  (3136 shorter events, 1272.3 us)
Async XLA Ops:
  0.6 79.0 %copy-start = (f32[64,64]{1,0:T(8,128)S(1)}, f32[64,64]{1,0:T(8,128)}, u32[]{:S(2)}) copy-start(f32[64,64]{1,0:T(8,128)} %param.36) | copy-start | bytes 49156
  1.7 0.8 copy-start.1
  1.7 0.8 copy-start.2
  1.7 0.8 copy-start.4
  1.7 0.7 copy-start.5
  1.8 0.7 copy-start.9
  62.6 24.6 all-to-all-start.2
  77.6 0.7 copy-start.7
  87.3 15.1 all-to-all-start
  93.1 0.7 copy-start.8
  93.7 0.7 copy-start.6
  103.1 0.7 copy-start.3
  2181.7 14.1 all-to-all-start.3
  2195.8 106.7 %all-to-all-start.1 = ((f32[64,1,128]{2,1,0:T(1,128)}), f32[64,1,128]{2,1,0:T(1,128)S(1)}, u32[]{:S(2)}, u32[]{:S(2)}) async-start(f32[64,1,128]{2,1,0:T(1,128)} %reshape.346), calls=%async_computation.1 | async-start | bytes 65536 | tf_op jit(solution)/shard_map/all_to_all | solution.py:191
where the time goes:
time: 2490 us; the launch traced here: 2470 us
  loops' own time  1010 us (41%)
  other arithmetic  511 us (21%)
  local copies, waits for them, and re-layouts  448 us (18%)
  matrix products  336 us (13%)
  blocking collectives  112 us (4%)
  starting transfers between devices  30 us (1%)
    another operation x2, loops' own time, descend(): return lax.fori_loop(0, edge_count, descend_visit, (outside, totals))  719 us
    another operation x2, loops' own time, climb_tree(): lax.fori_loop(0, edge_count, climb_visit, (inside, log_scale))  291 us
    mul x140, other arithmetic, integrals(): return branch * jnp.exp(eig_values[None, :] * branch) * growth  169 us
    dot_general x140, matrix products, descend_visit(): jnp.dot(count_basis * integrals(eig_values, branch), projected, precision...  139 us
    scatter x140, other arithmetic, descend_visit(): return (outside, totals.at[position].set(pattern_total))  113 us
    psum x1, blocking collectives, on_device(): top_sum = lax.psum(top_totals, ('leaf', 'site'))  99.4 us
    exp x140, other arithmetic, propagate(): damping = jnp.exp(eig_values * branch)  96.4 us
    dynamic_slice x140, local copies, waits for them, and re-layouts, climb_visit(): parent_node = tree_links[position]  95.9 us
  transfers between devices with their start and end apart: 4, of which 3 were waited for; matrix products, arithmetic and copies ran while one was open for 0% of the time, Pallas kernels for 0%

commit v1 on v0

v1 whole, which is shorter than its diff:
```python
import functools

import jax
import jax.numpy as jnp
from jax import lax
from jax.experimental import pallas as pl
from jax.experimental.pallas import tpu as pltpu
from jax.sharding import PartitionSpec as P

CODONS = 61
S = 64
T = 128
LEAVES = 8
LOC = 14
GROUPS = 64
TOP = 126
ROOT = 126
WIN = 4
F32 = jnp.float32
BF16 = jnp.bfloat16
PRECISE = lax.Precision.HIGHEST


def split(u):
    high = u.astype(BF16)
    low = (u - high.astype(F32)).astype(BF16)
    return high, low


def apply(w, u):
    high, low = split(u)
    return jnp.dot(w, jnp.concatenate([high, low, high, low], axis=0), preferred_element_type=F32)


def pack(doubled):
    high, low = split(doubled)
    return jnp.concatenate([high, low], axis=1)


def dot(a, b):
    return jnp.dot(a, b, precision=PRECISE, preferred_element_type=F32)


def growth(x):
    series = 1.0 + x * (1 / 2 + x * (1 / 6 + x * (1 / 24 + x * (1 / 120 + x * (
        1 / 720 + x * (1 / 5040 + x * (1 / 40320)))))))
    small = jnp.abs(x) < 0.5
    safe = jnp.where(small, 1.0, x)
    return jnp.where(small, series, (jnp.exp(x) - 1.0) / safe)


def iota(shape, axis):
    return lax.broadcasted_iota(jnp.int32, shape, axis)


def column(row):
    eye = iota((S, S), 0) == iota((S, S), 1)
    return jnp.sum(jnp.where(eye, row, 0.0), axis=1, keepdims=True)


def biggest(u):
    inside = iota((S, T), 0) < CODONS
    return jnp.max(jnp.where(inside, u, 0.0), axis=0, keepdims=True)


def inverse(row):
    return pltpu.reciprocal(row, approx=True)


def integral_matrix(vectors, inverse_vectors, basis, lam_row, lam_col, t):
    spread = (lam_col - lam_row) * t
    held = basis * (t * jnp.exp(lam_row * t) * growth(spread))
    return dot(dot(vectors, held), jnp.concatenate([inverse_vectors, inverse_vectors], axis=1))


def local_children(parents, node):
    late, early = jnp.int32(0), jnp.int32(0)
    for c in range(LOC):
        hit = parents[c] == node
        early = jnp.where(hit, late, early)
        late = jnp.where(hit, c, late)
    return late, early


def prepare(parents, lengths, top_lengths, tips, vectors, inverse_vectors, lam, rates,
            sent, w_top, w_loc, m_loc, y_loc, expo, x_int):
    me = lax.axis_index("leaf")
    lam_row = lam[...]
    lam_col = column(lam_row)
    lam2 = jnp.concatenate([lam_row, lam_row], axis=1)
    used = iota((S, S), 0) < CODONS
    right = jnp.where(used, vectors[...], 0.0)
    left = inverse_vectors[...]
    right2 = jnp.concatenate([right, right], axis=1)
    left2 = jnp.concatenate([left, left], axis=1)
    left_high, left_low = split(left2)
    left_stack = jnp.concatenate([left_high, left_low, left_high, left_low], axis=0)
    r2, c2 = iota((S, T), 0), iota((S, T), 1)
    eye2 = jnp.where((r2 < CODONS) & ((r2 == c2) | (r2 + S == c2)), 1.0, 0.0)

    def branch(t):
        x = lam2 * t
        scaled = right2 * (x * growth(x))
        return pack(eye2 + jnp.dot(pack(scaled), left_stack, preferred_element_type=F32))

    for c in range(LOC):
        w_loc[c] = branch(lengths[c])
    w_loc[LOC] = branch(top_lengths[me])

    for c in range(LEAVES):
        m_loc[c] = apply(w_loc[c], tips[c])
    factors = []
    for n in range(LEAVES, LOC + 1):
        a, b = local_children(parents, n)
        u = m_loc[a] * m_loc[b]
        r = inverse(biggest(u))
        factors.append(r)
        x_int[n - LEAVES] = u * r
        y = apply(w_loc[n], u) * r
        if n < LOC:
            m_loc[n] = y
        else:
            logs = -jnp.sum(jnp.log(jnp.concatenate(factors, axis=0)), axis=0, keepdims=True)
            sent[...] = jnp.where(iota((S, T), 0) == S - 1, logs, y)

    basis = dot(dot(left, rates[...]), right)
    for c in range(LOC + 1):
        t = lengths[c] if c < LOC else top_lengths[me]
        n_c = integral_matrix(right, left, basis, lam_row, lam_col, t)
        y_loc[c] = apply(pack(n_c), tips[c] if c < LEAVES else x_int[c - LEAVES])

    def top_branch(i, _):
        w_top[i] = branch(top_lengths[GROUPS + i])
        return 0

    lax.fori_loop(0, TOP - GROUPS, top_branch, 0)
    for i in range(TOP - GROUPS, TOP - GROUPS + WIN):
        w_top[i] = jnp.zeros((S, 256), BF16)


def joining(top_parents, parents, top_lengths, gathered, w_top, w_loc, m_loc, y_loc, weights, vectors,
            inverse_vectors, lam, rates, freq, out, late, early, path, msg, factor, arrs, o_loc, rows, sem):
    copy = pltpu.make_async_copy(gathered, msg.at[pl.ds(0, GROUPS)], sem)
    copy.start()
    me = lax.axis_index("leaf")

    def link(c, _):
        p = top_parents[c]
        early[p] = late[p]
        late[p] = c
        return 0

    for i in range(GROUPS, ROOT + 1 + WIN):
        late[i] = 0
        early[i] = 0
    lax.fori_loop(0, TOP, link, 0, unroll=2)
    factor[...] = jnp.ones((72, T), F32)
    copy.wait()
    local_logs = msg[0, pl.ds(S - 1, 1)]
    for g in range(1, GROUPS):
        local_logs += msg[g, pl.ds(S - 1, 1)]

    def climb(n):
        done = []
        fits = True
        steps = jnp.int32(1)
        for j in range(WIN):
            a, b = late[n + j], early[n + j]
            if j:
                fits = fits & (a < n)
                steps = steps + fits.astype(jnp.int32)
            u = msg[a] * msg[b]
            y = apply(w_top[n + j - GROUPS], u)
            r = inverse(biggest(u))
            done.append((y * r, r))
        for j, (y, r) in enumerate(done):
            msg[n + j] = y
            factor[pl.ds(n + j - GROUPS, 1)] = r
        return n + steps

    lax.while_loop(lambda n: n < ROOT, climb, jnp.int32(GROUPS))

    freq_col = column(freq[...])
    root_u = msg[late[ROOT]] * msg[early[ROOT]]
    likelihood = jnp.sum(freq_col * root_u, axis=0, keepdims=True)
    row = iota((72, T), 0)
    top_logs = -jnp.sum(jnp.log(jnp.where(row < TOP - GROUPS, factor[...], 1.0)), axis=0, keepdims=True)
    loglik = (jnp.log(likelihood) + top_logs + local_logs) * (1.0 / (GROUPS * LEAVES))

    def walk(state):
        c, depth, mine, at = state
        path[depth] = c
        p = top_parents[c]
        found = (mine < 0) & (late[p] == c)
        return (p, depth + 1, jnp.where(found, p, mine), jnp.where(found, depth + 1, at))

    _, depth, mine, at = lax.while_loop(
        lambda state: state[0] != ROOT, walk, (me, jnp.int32(0), jnp.int32(-1), jnp.int32(0)))
    counted = (mine >= 0) & (mine < ROOT)
    node = jnp.where(counted, mine, GROUPS)
    at = jnp.where(counted, at, 0)

    def step_down(i, o):
        k = depth - 1 - i
        c = path[k]
        p = top_parents[c]
        arriving = o * msg[late[p] + early[p] - c]
        arrs[k] = arriving
        w = w_top[c - GROUPS]
        return apply(w, arriving) * inverse(biggest(arriving))

    o = lax.fori_loop(0, depth - 1, step_down, jnp.ones((S, T), F32))
    p = top_parents[me]
    arriving = o * msg[late[p] + early[p] - me]
    arrs[0] = arriving
    o_loc[LOC - LEAVES] = apply(w_loc[LOC], arriving) * inverse(biggest(arriving))

    def ratio(slot, arriving, message, y):
        weighted = freq_col * arriving
        rows[0, pl.ds(slot, 1)] = jnp.sum(weighted * y, axis=0, keepdims=True)
        rows[1, pl.ds(slot, 1)] = jnp.sum(weighted * message, axis=0, keepdims=True)

    rows[...] = jnp.ones((2, 24, T), F32)
    ratio(16, arriving, msg[me], y_loc[LOC])
    lam_row = lam[...]
    used = iota((S, S), 0) < CODONS
    right = jnp.where(used, vectors[...], 0.0)
    left = inverse_vectors[...]
    basis = dot(dot(left, rates[...]), right)
    n_c = integral_matrix(right, left, basis, lam_row, column(lam_row), top_lengths[node])
    u = msg[late[node]] * msg[early[node]]
    ratio(17, arrs[at], msg[node], apply(pack(n_c), u) * factor[pl.ds(node - GROUPS, 1)])

    for c in range(LOC - 1, -1, -1):
        p = parents[c]
        sibling = jnp.int32(0)
        for other in range(LOC):
            if other != c:
                sibling = jnp.where(parents[other] == p, other, sibling)
        arriving = o_loc[p - LEAVES] * m_loc[sibling]
        if c >= LEAVES:
            o_loc[c - LEAVES] = apply(w_loc[c], arriving) * inverse(biggest(arriving))
        ratio(c, arriving, m_loc[c], y_loc[c])

    weight = weights[...].astype(F32)
    expected = weight * rows[0] / rows[1]
    slot = iota((24, T), 0)
    expected = jnp.where(slot == LOC, weight, expected)
    sums = lax.dot_general(jnp.ones((8, T), F32), expected, (((1,), (1,)), ((), ())),
                           precision=PRECISE, preferred_element_type=F32)
    lane = iota((1, T), 1)
    own = sums[0:1, 16:17]
    inner = sums[0:1, 17:18]
    top_row = jnp.where(lane == me, own, 0.0) + jnp.where((lane == node) & counted, inner, 0.0)
    out[...] = jnp.zeros((8, T), F32)
    out[pl.ds(0, 1), pl.ds(0, 24)] = sums[0:1]
    out[pl.ds(1, 1)] = top_row
    out[pl.ds(2, 1)] = loglik


def on_device(tips, parents, branch_lengths, top_parents, top_lengths, weights, eig_vectors,
              eig_inverse, eig_values, labeled_rates, root_freq):
    smem = pl.BlockSpec(memory_space=pltpu.SMEM)
    vmem = pl.BlockSpec(memory_space=pltpu.VMEM)
    params = pltpu.CompilerParams(vmem_limit_bytes=40 << 20)
    lam = eig_values.reshape(1, S)
    freq = root_freq.reshape(1, S)
    sent, w_top, w_loc, m_loc, y_loc = pl.pallas_call(
        prepare,
        out_shape=(
            jax.ShapeDtypeStruct((S, T), F32),
            jax.ShapeDtypeStruct((TOP - GROUPS + WIN, S, 256), BF16),
            jax.ShapeDtypeStruct((LOC + 1, S, 256), BF16),
            jax.ShapeDtypeStruct((LOC, S, T), F32),
            jax.ShapeDtypeStruct((LOC + 1, S, T), F32),
        ),
        in_specs=[smem] * 3 + [vmem] * 5,
        out_specs=(vmem,) * 5,
        scratch_shapes=[pltpu.VMEM((8, T), F32), pltpu.VMEM((8, S, T), F32)],
        compiler_params=params,
        name="prepare",
    )(parents, branch_lengths, top_lengths, tips, eig_vectors, eig_inverse, lam, labeled_rates)
    gathered = lax.all_gather(sent, "leaf")
    out = pl.pallas_call(
        joining,
        out_shape=jax.ShapeDtypeStruct((8, T), F32),
        in_specs=[smem] * 3 + [pl.BlockSpec(memory_space=pl.ANY)] + [vmem] * 10,
        out_specs=vmem,
        scratch_shapes=[
            pltpu.SMEM((136,), jnp.int32),
            pltpu.SMEM((136,), jnp.int32),
            pltpu.SMEM((64,), jnp.int32),
            pltpu.VMEM((ROOT + 1 + WIN, S, T), F32),
            pltpu.VMEM((72, T), F32),
            pltpu.VMEM((GROUPS, S, T), F32),
            pltpu.VMEM((8, S, T), F32),
            pltpu.VMEM((2, 24, T), F32),
            pltpu.SemaphoreType.DMA,
        ],
        compiler_params=params,
        name="joining",
    )(top_parents, parents, top_lengths, gathered, w_top, w_loc, m_loc, y_loc, weights.reshape(1, T),
      eig_vectors, eig_inverse, lam, labeled_rates, freq)
    local_sum = lax.psum(out[0, :LOC + 1], "site")
    top_sum = lax.psum(out[1], ("leaf", "site"))
    total = local_sum[LOC]
    return local_sum[:LOC] / total, top_sum[:TOP] / total, out[2]


def solution(mesh):
    placed = (P("leaf", None, "site"), P("leaf"), P("leaf"), P(), P(), P("site"), P(), P(), P(), P(), P())
    return jax.shard_map(
        on_device,
        mesh=mesh,
        in_specs=placed,
        out_specs=(P("leaf"), P(), P("site")),
        check_vma=False,
    )
```

time: 2490 us -> 259 us (0.10)
  loops' own time: 1010 us -> 0 us
  other arithmetic: 511 us -> 2.41 us
  local copies, waits for them, and re-layouts: 448 us -> 16.6 us
  matrix products: 336 us -> 0 us
  waiting for transfers between devices: 19.9 us -> 89.4 us
  starting transfers between devices: 30 us -> 0.04 us
    another operation x4 -> x0, loops' own time: 1010 us -> none  [the longest x2 719 us: descend(): return lax.fori_loop(0, edge_count, descend_visit, (outside, totals))]
    dynamic_slice x841 -> x0, local copies, waits for them, and re-layouts: 437 us -> none  [the longest x140 95.9 us: climb_visit(): parent_node = tree_links[position]]
    dot_general x1122 -> x0, matrix products: 336 us -> none  [the longest x140 139 us: descend_visit(): jnp.dot(count_basis * integrals(eig_values, branch), projected, precision...]
    mul x141 -> x0, other arithmetic: 170 us -> none  [the longest x140 169 us: integrals(): return branch * jnp.exp(eig_values[None, :] * branch) * growth]
    scatter x140 -> x0, other arithmetic: 113 us -> none  [descend_visit(): return (outside, totals.at[position].set(pattern_total))]
    exp x140 -> x0, other arithmetic: 96.4 us -> none  [propagate(): damping = jnp.exp(eig_values * branch)]
    all_gather x0 -> x1, waiting for transfers between devices: none -> 89.4 us  [on_device(): gathered = lax.all_gather(sent, 'leaf')]
    reduce_sum x145 -> x0, other arithmetic: 87.4 us -> none  [the longest x140 86.4 us: descend_visit(): pattern_total = jnp.sum(weight * numerator / denominator)]
  transfers between devices with their start and end apart: 4 -> 1, of which waited for: 3 -> 1; matrix products, arithmetic and copies ran while one was open for 0% -> 0% of each run, Pallas kernels for 0% -> 0%
where the time goes in v1:
time: 259 us; the launch traced here: 258 us
  blocking collectives  112 us (43%)
  waiting for transfers between devices  89.4 us (35%)
  Pallas kernels  24 us (9%)
  local copies, waits for them, and re-layouts  16.6 us (6%)
  between operations  14.1 us (5%)
    psum x1, blocking collectives, on_device(): top_sum = lax.psum(out[1], ('leaf', 'site'))  98.4 us
    all_gather x1, waiting for transfers between devices, on_device(): gathered = lax.all_gather(sent, 'leaf')  89.4 us
    pallas_call x1, Pallas kernels, on_device(): pl.pallas_call(prepare, out_shape=(jax.ShapeDtypeStruct((S, T), F32), jax...  15.7 us
    unnamed x40, local copies, waits for them, and re-layouts  15.4 us
    psum x1, blocking collectives, on_device(): local_sum = lax.psum(out[0, :LOC + 1], 'site')  13.2 us
    pallas_call x1, Pallas kernels, on_device(): pl.pallas_call(joining, out_shape=jax.ShapeDtypeStruct((8, T), F32), in_s...  8.31 us
  transfers between devices with their start and end apart: 1, of which 1 were waited for; matrix products, arithmetic and copies ran while one was open for 0% of the time, Pallas kernels for 0%

profile of v1, /device:TPU:1, one launch (start us, length us, event | category | flops | bytes accessed | tf_op | source)
XLA Modules:
  0.0 258.2 jit_solution(8055522465453710633)
XLA Ops:
  7.2 0.0 all-gather.3.cloned.1.call-start
  7.2 0.0 copy-start.3
  7.2 0.9 copy-done.3
  8.2 0.8 copy-done.4
  8.9 0.8 copy-done.6
  9.7 0.8 copy-done.8
  10.4 0.7 copy-done.10
  11.1 0.7 copy-done.12
  11.8 0.7 copy-done.14
  12.4 0.7 copy-done.16
  13.1 15.7 %prepare.1 = (f32[64,128]{1,0:T(8,128)}, bf16[66,64,256]{2,1,0:T(8,128)(2,1)S(1)}, bf16[15,64,256]{2,1,0:T(8,128)(2,1)S(1)}, f32[14,64,128]{2,1,0:T(8,128)S(1)}, f32[15,64,128]{2,1,0:T(8,128)S(1)}) custom-call(s32[14]{0:T(128)S(1)} %copy-done.10, f32[14]{0:T(128)S(1)} %copy-done.16, f32[126]{0:T(128)S(1)} %copy-done.12, f32[8,64,128]{2,1,0:T(8,128)S(1)} %copy-done.3, ...), custom_call_target="tpu_custom_call" | custom-call | tf_op jit(solution)/shard_map/prepare/pallas_call | solution.py:268
  28.7 0.8 copy-done.1
  29.5 0.0 all-gather.3.cloned.1.call-update
  29.5 89.4 %all-gather.3.cloned.1.call-done = f32[4096,128]{1,0:T(8,128)} async-done(((f32[64,128]{1,0:T(8,128)}), f32[4096,128]{1,0:T(8,128)}) %all-gather.3.cloned.1.call-update) | async-done | bytes 2097168 | tf_op jit(solution)/shard_map/all_gather | solution.py:283
  119.0 1.6 copy-done
  120.6 1.0 copy-done.2
  121.6 0.8 copy-done.5
  122.3 0.8 copy-done.7
  123.1 0.8 copy-done.9
  123.8 0.7 copy-done.11
  124.5 0.7 copy-done.13
  125.2 0.7 copy-done.15
  125.8 0.7 copy-done.17
  126.5 0.7 copy-done.18
  127.1 0.7 copy-done.19
  127.8 8.3 %joining.1 = f32[8,128]{1,0:T(8,128)S(1)} custom-call(s32[126]{0:T(128)S(1)} %copy-done.17, s32[14]{0:T(128)S(1)} %copy-done.11, f32[126]{0:T(128)S(1)} %copy-done.13, f32[64,64,128]{2,1,0:T(8,128)S(1)} %bitcast.11, bf16[66,64,256]{2,1,0:T(8,128)(2,1)S(1)} %get-tuple-element.9.w_top, bf16[15,64,256]{2,1,0:T(8,128)(2,1)S(1)} %get-tuple-element.10.w_loc, ...), custom_call_target="tpu_custom_call" | custom-call | tf_op jit(solution)/shard_map/joining/pallas_call | solution.py:284
  136.1 0.5 slice_bitcast_fusion
  136.6 13.2 %psum.14 = f32[15]{0:T(128)S(1)} all-reduce(f32[15]{0:T(128)S(1)} %slice_bitcast_fusion.2), channel_id=1, replica_groups=mesh['leaf'=64,'site'=8] {'site'}, use_global_device_ids=true, to_apply=%region_0.0 | all-reduce | flops 15 | bytes 120 | tf_op jit(solution)/shard_map/psum | solution.py:304
  149.8 0.7 slice.20
  150.5 1.2 slice_divide_fusion.1
  151.7 98.4 %psum.15 = f32[128]{0:T(128)S(1)} all-reduce(f32[128]{0:T(128)S(1)} %get-tuple-element.14), channel_id=1, replica_groups=mesh['leaf'=64,'site'=8] {'leaf','site'}, use_global_device_ids=true, to_apply=%region_1.0 | all-reduce | flops 128 | bytes 1024 | tf_op jit(solution)/shard_map/psum | solution.py:305
  250.1 1.2 slice_divide_fusion
  (20 shorter events, 0.0 us)
Async XLA Ops:
  7.2 111.8 %all-gather.3.cloned.1.call-start = ((), (), s32[]{:S(2)}) async-start(), calls=%async_computation | async-start | bytes 2129920 | tf_op jit(solution)/shard_map/all_gather | solution.py:283
  7.2 1.0 copy-start.3
  8.2 0.8 copy-start.4
  8.9 0.8 copy-start.6
  9.7 0.8 copy-start.8
  10.4 0.7 copy-start.10
  11.1 0.7 copy-start.12
  11.7 0.7 copy-start.14
  12.4 0.7 copy-start.16
  28.7 0.8 copy-start.1
  119.0 1.6 copy-start
  120.6 1.0 copy-start.2
  121.6 0.8 copy-start.5
  122.3 0.8 copy-start.7
  123.1 0.8 copy-start.9
  123.8 0.7 copy-start.11
  124.5 0.7 copy-start.13
  125.2 0.7 copy-start.15
  125.8 0.7 copy-start.17
  126.5 0.7 copy-start.18
  127.1 0.7 copy-start.19
Sparse Core Ops, SparseCore 0:
  29.7 89.2 all-gather.2

commit v2 on v1

v2 whole, which is shorter than its diff:
```python
import functools

import jax
import jax.numpy as jnp
from jax import lax
from jax.experimental import pallas as pl
from jax.experimental.pallas import tpu as pltpu
from jax.sharding import PartitionSpec as P

CODONS = 61
S = 64
T = 128
LEAVES = 8
LOC = 14
GROUPS = 64
TOP = 126
ROOT = 126
WIN = 4
NX, NZ, NY = 4, 8, 8
CUT = 40
HOPS = ((1, 4), (-1, 3))
F32 = jnp.float32
BF16 = jnp.bfloat16
PRECISE = lax.Precision.HIGHEST
MESH = pl.DeviceIdType.MESH


def split(u):
    high = u.astype(BF16)
    low = (u - high.astype(F32)).astype(BF16)
    return high, low


def apply(w, u):
    high, low = split(u)
    return jnp.dot(w, jnp.concatenate([high, low, high, low], axis=0), preferred_element_type=F32)


def pack(doubled):
    high, low = split(doubled)
    return jnp.concatenate([high, low], axis=1)


def double(a):
    return jnp.concatenate([a, a], axis=1)


def dot(a, b):
    return jnp.dot(a, b, precision=PRECISE, preferred_element_type=F32)


def growth(x):
    series = 1.0 + x * (1 / 2 + x * (1 / 6 + x * (1 / 24 + x * (1 / 120 + x * (
        1 / 720 + x * (1 / 5040 + x * (1 / 40320)))))))
    small = jnp.abs(x) < 0.5
    safe = jnp.where(small, 1.0, x)
    return jnp.where(small, series, (jnp.exp(x) - 1.0) / safe)


def iota(shape, axis):
    return lax.broadcasted_iota(jnp.int32, shape, axis)


def column(row):
    n = row.shape[1]
    eye = iota((n, n), 0) == iota((n, n), 1)
    return jnp.sum(jnp.where(eye, row, jnp.zeros_like(row)), axis=1, keepdims=True)


def biggest(u):
    used = iota((S, T), 0) < CODONS
    return jnp.max(jnp.where(used, u, 0.0), axis=0, keepdims=True)


def inverse(row):
    return pltpu.reciprocal(row, approx=True)


def held_integrals(basis2, lam2, lam_col, t):
    spread = (lam_col - lam2) * t
    return pack(basis2 * (t * jnp.exp(lam2 * t) * growth(spread)))


def local_children(parents, node):
    late, early = jnp.int32(0), jnp.int32(0)
    for c in range(LOC):
        hit = parents[c] == node
        early = jnp.where(hit, late, early)
        late = jnp.where(hit, c, late)
    return late, early


def slot_of(x, z, c):
    return c * (NX * NZ) + z * NX + x


def prepare(parents_h, lengths_h, top_lengths_h, top_parents_h, tips_h, vectors_h, inverse_h, lam_h, rates_h, freq_h,
            msg, w_top, w_loc, m_loc, y_loc, links, eig_w, inv_w, basis_out, lam_out, freq_out,
            parents, lengths, top_lengths, top_parents, tips, vectors, inverse_vectors, lam, rates, freq, x_int,
            in_sem, send_sem, recv_sem):
    me = lax.axis_index("leaf")
    site = lax.axis_index("site")
    core = lax.rem(me, 2)
    z = lax.rem(me // 2, NZ)
    x = me // (2 * NZ)

    loads = [pltpu.make_async_copy(src, dst, in_sem.at[i]) for i, (src, dst) in enumerate((
        (vectors_h, vectors), (inverse_h, inverse_vectors), (lam_h, lam), (lengths_h, lengths),
        (top_lengths_h, top_lengths), (tips_h, tips), (parents_h, parents), (rates_h, rates),
        (top_parents_h, top_parents), (freq_h, freq)))]
    for load in loads:
        load.start()

    def device(dx, dz, dc):
        nx, nz = lax.rem(x + dx + NX, NX), lax.rem(z + dz + NZ, NZ)
        nc = 1 - core if dc else core
        return ((nx * NZ + nz) * 2 + nc, site)

    x_peers = [(dx, 0, 0) for dx in (1, 2, 3)]
    partners = x_peers + [(0, 1, 0), (0, -1, 0), (0, 0, 1)]
    barrier = pltpu.get_barrier_semaphore()
    for partner in partners:
        pl.semaphore_signal(barrier, inc=1, device_id=device(*partner), device_id_type=MESH)

    for load in loads[:5]:
        load.wait()
    lam_row = lam[...]
    lam_col = column(lam_row)
    lam2 = double(lam_row)
    used = iota((S, S), 0) < CODONS
    right = jnp.where(used, vectors[...], 0.0)
    left = inverse_vectors[...]
    right2 = double(right)
    left_high, left_low = split(double(left))
    left_stack = jnp.concatenate([left_high, left_low, left_high, left_low], axis=0)
    r2, c2 = iota((S, T), 0), iota((S, T), 1)
    eye2 = jnp.where((r2 < CODONS) & ((r2 == c2) | (r2 + S == c2)), 1.0, 0.0)

    def branches(ts):
        scaled = []
        for t in ts:
            arg = lam2 * t
            scaled.append(pack(right2 * (arg * growth(arg))))
        result = jnp.dot(jnp.concatenate(scaled, axis=0), left_stack, preferred_element_type=F32)
        return [pack(eye2 + result[S * i:S * (i + 1)]) for i in range(len(ts))]

    for c, w in enumerate(branches([lengths[c] for c in range(LOC)] + [top_lengths[me]])):
        w_loc[c] = w

    loads[5].wait()
    loads[6].wait()
    for c in range(LEAVES):
        m_loc[c] = apply(w_loc[c], tips[c])
    factors = []
    for n in range(LEAVES, LOC + 1):
        a, b = local_children(parents, n)
        u = m_loc[a] * m_loc[b]
        r = inverse(biggest(u))
        factors.append(r)
        x_int[n - LEAVES] = u * r
        y = apply(w_loc[n], u) * r
        if n < LOC:
            m_loc[n] = y
        else:
            logs = -jnp.sum(jnp.log(jnp.concatenate(factors, axis=0)), axis=0, keepdims=True)
            msg[slot_of(x, z, core)] = jnp.where(iota((S, T), 0) == S - 1, logs, y)
    pl.semaphore_wait(barrier, len(partners))

    counter = [0]

    def own_piece(xs, zs, rows):
        if xs is None:
            return msg.at[pl.ds(slot_of(0, zs, core), NX), rows]
        return msg.at[slot_of(xs, zs, core), rows]

    def other_piece(zs, rows):
        return msg.at[pl.ds(slot_of(0, zs, 1 - core), NX), rows]

    started = []

    def send(piece, where, arriving):
        k = counter[0]
        counter[0] += 1
        copy = pltpu.make_async_remote_copy(src_ref=piece, dst_ref=piece, send_sem=send_sem.at[k],
                                            recv_sem=recv_sem.at[k], device_id=device(*where), device_id_type=MESH)
        copy.start()
        started.append(copy)
        incoming = pltpu.make_async_remote_copy(src_ref=arriving, dst_ref=arriving, send_sem=send_sem.at[k],
                                                recv_sem=recv_sem.at[k], device_id=device(*where), device_id_type=MESH)
        return incoming

    first, second = pl.ds(0, CUT), pl.ds(CUT, S - CUT)

    def at_z(dz):
        return lax.rem(z + dz + NZ, NZ)

    def at_x(dx):
        return lax.rem(x + dx + NX, NX)

    def spread_x(dz):
        return [send(own_piece(x, at_z(dz), first), (dx, 0, 0), own_piece(at_x(-dx), at_z(dz), first))
                for dx in (1, 2, 3)]

    def cross(dz, rows):
        return send(own_piece(None, at_z(dz), rows), (0, 0, 1), other_piece(at_z(dz), rows))

    def hop_first(direction, h):
        return send(own_piece(x, at_z(-direction * (h - 1)), first), (0, direction, 0),
                    own_piece(x, at_z(-direction * h), first))

    def hop_second(direction, h):
        return send(own_piece(None, at_z(-direction * (h - 1)), second), (0, direction, 0),
                    own_piece(None, at_z(-direction * h), second))

    def work(stage):
        if stage == 0:
            loads[7].wait()
            loads[8].wait()
            loads[9].wait()
            parent_col = column(top_parents[...])
            child = iota((TOP, T), 0)
            hit = parent_col == iota((TOP, T), 1)
            late = jnp.max(jnp.where(hit, child, 0), axis=0, keepdims=True)
            early = jnp.min(jnp.where(hit, child, TOP), axis=0, keepdims=True)
            pair = jnp.concatenate([late, early, jnp.zeros((6, T), jnp.int32)], axis=0)
            slots = (pair & 1) * (NX * NZ) + ((pair >> 1) & (NZ - 1)) * NX + (pair >> 4)
            pair = jnp.where(pair < GROUPS, slots, pair)
            lane = iota((8, T), 1)
            links[...] = jnp.where((lane >= GROUPS) & (lane <= ROOT), pair, 0)
            freq_out[...] = jnp.broadcast_to(column(freq[...]), (S, T))
            lam_out[...] = jnp.broadcast_to(lam2, (8, T))
            basis_out[...] = double(dot(dot(left, rates[...]), right))
            eig_w[...] = pack(right2)
            inv_w[...] = pack(double(left))
        elif stage <= 4:
            per = 4
            for c in range((stage - 1) * per, min(stage * per, LOC + 1)):
                t = lengths[c] if c < LOC else top_lengths[me]
                v = apply(inv_w[...], tips[c] if c < LEAVES else x_int[c - LEAVES])
                y_loc[c] = apply(eig_w[...], apply(held_integrals(basis_out[...], lam2, lam_col, t), v))
        else:
            lo, hi = ((0, 4), (4, 8))[stage - 5]

            def some(i, _):
                for j, w in enumerate(branches([top_lengths[jnp.minimum(GROUPS + i * 8 + j, TOP - 1)] for j in range(8)])):
                    w_top[i * 8 + j] = w
                return 0

            lax.fori_loop(lo, hi, some, 0)

    x_second = [send(own_piece(x, z, second), (dx, 0, 0), own_piece(at_x(-dx), z, second)) for dx in (1, 2, 3)]
    z_first = {d: hop_first(d, 1) for d, _ in HOPS}
    spreads = [(0, spread_x(0))]
    crossed = []
    work(0)
    for incoming in x_second:
        incoming.wait_recv()
    z_second = {d: hop_second(d, 1) for d, _ in HOPS}
    crossed.append(cross(0, second))
    for h in range(1, 5):
        work(h)
        for d, most in HOPS:
            if h > most:
                continue
            z_first[d].wait_recv()
            if h < most:
                z_first[d] = hop_first(d, h + 1)
            spreads.append((-d * h, spread_x(-d * h)))
        for d, most in HOPS:
            if h > most:
                continue
            z_second[d].wait_recv()
            if h < most:
                z_second[d] = hop_second(d, h + 1)
            crossed.append(cross(-d * h, second))
        ready, spreads = spreads[:-2], spreads[-2:]
        for dz, incoming in ready:
            for one in incoming:
                one.wait_recv()
            crossed.append(cross(dz, first))
    work(5)
    for dz, incoming in spreads:
        for one in incoming:
            one.wait_recv()
        crossed.append(cross(dz, first))
    work(6)
    for one in crossed:
        one.wait_recv()
    for one in started:
        one.wait_send()


COPIES = 3 + 7 + 24 + 7 + 16


def joining(top_parents_h, parents_h, top_lengths_h, weights_h, links, msg_in, w_top, w_loc, m_loc, y_loc,
            eig_w, inv_w, basis, lam, freq, out, msg,
            top_parents, parents, top_lengths, weights, path, factor, arrs, o_loc, rows, sem):
    del msg_in
    loads = [pltpu.make_async_copy(src, dst, sem.at[i]) for i, (src, dst) in enumerate((
        (top_parents_h, top_parents), (parents_h, parents), (top_lengths_h, top_lengths), (weights_h, weights)))]
    for load in loads:
        load.start()
    me = lax.axis_index("leaf")
    slot = slot_of(me // (2 * NZ), lax.rem(me // 2, NZ), lax.rem(me, 2))
    factor[...] = jnp.ones((72, T), F32)
    local_logs = msg[0, pl.ds(S - 1, 1)]
    for g in range(1, GROUPS):
        local_logs += msg[g, pl.ds(S - 1, 1)]

    def late(n):
        return links[0, n]

    def early(n):
        return links[1, n]

    def climb(n):
        done = []
        fits = True
        steps = jnp.int32(1)
        for j in range(WIN):
            k = jnp.minimum(n + j, T - 1) if j > 1 else n + j
            a, b = late(k), early(k)
            if j:
                fits = fits & (a < n)
                steps = steps + fits.astype(jnp.int32)
            u = msg[a] * msg[b]
            y = apply(w_top[jnp.minimum(k, ROOT) - GROUPS], u)
            r = inverse(biggest(u))
            done.append((y * r, r))
        for j, (y, r) in enumerate(done):
            msg[n + j] = y
            factor[pl.ds(n + j - GROUPS, 1)] = r
        return n + steps

    lax.while_loop(lambda n: n < ROOT, climb, jnp.int32(GROUPS))

    freq_col = freq[...]
    root_u = msg[late(ROOT)] * msg[early(ROOT)]
    likelihood = jnp.sum(freq_col * root_u, axis=0, keepdims=True)
    row = iota((72, T), 0)
    top_logs = -jnp.sum(jnp.log(jnp.where(row < TOP - GROUPS, factor[...], 1.0)), axis=0, keepdims=True)
    loglik = (jnp.log(likelihood) + top_logs + local_logs) * (1.0 / (GROUPS * LEAVES))
    for load in loads:
        load.wait()

    def walk(state):
        c, depth, mine, at = state
        path[depth] = c
        p = top_parents[jnp.where(depth == 0, me, c)]
        found = (mine < 0) & (late(p) == c)
        return (p, depth + 1, jnp.where(found, p, mine), jnp.where(found, depth + 1, at))

    _, depth, mine, at = lax.while_loop(
        lambda state: state[0] != ROOT, walk, (slot, jnp.int32(0), jnp.int32(-1), jnp.int32(0)))
    counted = (mine >= 0) & (mine < ROOT)
    node = jnp.where(counted, mine, GROUPS)
    at = jnp.where(counted, at, 0)

    def step_down(i, o):
        k = depth - 1 - i
        c = path[k]
        p = top_parents[c]
        arriving = o * msg[late(p) + early(p) - c]
        arrs[k] = arriving
        return apply(w_top[c - GROUPS], arriving) * inverse(biggest(arriving))

    o = lax.fori_loop(0, depth - 1, step_down, jnp.ones((S, T), F32))
    p = top_parents[me]
    arriving = o * msg[late(p) + early(p) - slot]
    arrs[0] = arriving
    o_loc[LOC - LEAVES] = apply(w_loc[LOC], arriving) * inverse(biggest(arriving))

    def ratio(place, arriving, message, y):
        weighted = freq_col * arriving
        rows[0, pl.ds(place, 1)] = jnp.sum(weighted * y, axis=0, keepdims=True)
        rows[1, pl.ds(place, 1)] = jnp.sum(weighted * message, axis=0, keepdims=True)

    rows[...] = jnp.ones((2, 24, T), F32)
    ratio(16, arriving, msg[slot], y_loc[LOC])
    lam2 = lam[0:1]
    v = apply(inv_w[...], msg[late(node)] * msg[early(node)]) * factor[pl.ds(node - GROUPS, 1)]
    y = apply(eig_w[...], apply(held_integrals(basis[...], lam2, column(lam2[:, :S]), top_lengths[node]), v))
    ratio(17, arrs[at], msg[node], y)

    for c in range(LOC - 1, -1, -1):
        p = parents[c]
        sibling = jnp.int32(0)
        for other in range(LOC):
            if other != c:
                sibling = jnp.where(parents[other] == p, other, sibling)
        arriving = o_loc[p - LEAVES] * m_loc[sibling]
        if c >= LEAVES:
            o_loc[c - LEAVES] = apply(w_loc[c], arriving) * inverse(biggest(arriving))
        ratio(c, arriving, m_loc[c], y_loc[c])

    weight = weights[...].astype(F32)
    expected = weight * rows[0] / rows[1]
    place = iota((24, T), 0)
    expected = jnp.where(place == LOC, weight, expected)
    sums = lax.dot_general(jnp.ones((8, T), F32), expected, (((1,), (1,)), ((), ())),
                           precision=PRECISE, preferred_element_type=F32)
    lane = iota((1, T), 1)
    own = sums[0:1, 16:17]
    inner = sums[0:1, 17:18]
    top_row = jnp.where(lane == me, own, 0.0) + jnp.where((lane == node) & counted, inner, 0.0)
    out[...] = jnp.zeros((8, T), F32)
    out[pl.ds(0, 1), pl.ds(0, 24)] = sums[0:1]
    out[pl.ds(1, 1)] = top_row
    out[pl.ds(2, 1)] = loglik


def reduce(mine, out, near, partial, far, send_sem, recv_sem):
    me = lax.axis_index("leaf")
    y = lax.axis_index("site")
    ny = lax.axis_size("site")
    core = lax.rem(me, 2)
    z = lax.rem(me // 2, NZ)
    x = me // (2 * NZ)
    nears = [(dy, dc) for dy in range(ny) for dc in (0, 1) if (dy, dc) != (0, 0)]
    fars = [(dx, dz) for dx in range(NX) for dz in range(NZ) if (dx, dz) != (0, 0)]

    def near_at(dy, dc):
        return lax.rem(y + dy + ny, ny), (1 - core if dc else core)

    def far_at(dx, dz):
        return lax.rem(x + dx + NX, NX), lax.rem(z + dz + NZ, NZ)

    def near_device(dy, dc):
        ty, tc = near_at(dy, dc)
        return ((x * NZ + z) * 2 + tc, ty)

    def far_device(dx, dz):
        tx, tz = far_at(dx, dz)
        return ((tx * NZ + tz) * 2 + core, y)

    barrier = pltpu.get_barrier_semaphore()
    for where in nears:
        pl.semaphore_signal(barrier, inc=1, device_id=near_device(*where), device_id_type=MESH)
    for where in fars:
        pl.semaphore_signal(barrier, inc=1, device_id=far_device(*where), device_id_type=MESH)
    pl.semaphore_wait(barrier, len(nears) + len(fars))

    def near_slot(ty, tc):
        return ty * 2 + tc

    near[near_slot(y, core)] = mine[...]
    copies = []
    arrivals = []
    for k, (dy, dc) in enumerate(nears):
        here = near.at[near_slot(y, core)]
        copy = pltpu.make_async_remote_copy(src_ref=mine, dst_ref=here, send_sem=send_sem.at[k],
                                            recv_sem=recv_sem.at[k], device_id=near_device(dy, dc), device_id_type=MESH)
        copy.start()
        copies.append(copy)
        there = near.at[near_slot(*near_at(-dy, dc))]
        arrivals.append(pltpu.make_async_remote_copy(
            src_ref=there, dst_ref=there, send_sem=send_sem.at[k], recv_sem=recv_sem.at[k],
            device_id=near_device(dy, dc), device_id_type=MESH))
    for arrival in arrivals:
        arrival.wait_recv()
    local = near[core]
    top = near[0] + near[1]
    for i in range(1, ny):
        local = local + near[2 * i + core]
        top = top + (near[2 * i] + near[2 * i + 1])
    partial[...] = top
    far[x * NZ + z] = top
    base = len(nears)
    arrivals = []
    for k, (dx, dz) in enumerate(fars):
        copy = pltpu.make_async_remote_copy(src_ref=partial, dst_ref=far.at[x * NZ + z], send_sem=send_sem.at[base + k],
                                            recv_sem=recv_sem.at[base + k], device_id=far_device(dx, dz), device_id_type=MESH)
        copy.start()
        copies.append(copy)
        tx, tz = far_at(-dx, -dz)
        there = far.at[tx * NZ + tz]
        arrivals.append(pltpu.make_async_remote_copy(
            src_ref=there, dst_ref=there, send_sem=send_sem.at[base + k], recv_sem=recv_sem.at[base + k],
            device_id=far_device(dx, dz), device_id_type=MESH))
    for arrival in arrivals:
        arrival.wait_recv()
    top = far[0]
    for i in range(1, NX * NZ):
        top = top + far[i]
    total = local[0:1, LOC:LOC + 1]
    out[...] = mine[...]
    out[pl.ds(0, 1)] = local[0:1] / total
    out[pl.ds(1, 1)] = top[1:2] / total
    for copy in copies:
        copy.wait_send()


def on_device(tips, parents, branch_lengths, top_parents, top_lengths, weights, eig_vectors,
              eig_inverse, eig_values, labeled_rates, root_freq):
    hbm = pl.BlockSpec(memory_space=pltpu.HBM)
    smem = pl.BlockSpec(memory_space=pltpu.SMEM)
    vmem = pl.BlockSpec(memory_space=pltpu.VMEM)
    shape = jax.ShapeDtypeStruct
    msg, *made = pl.pallas_call(
        prepare,
        out_shape=(
            shape((ROOT + 1 + WIN, S, T), F32),
            shape((GROUPS, S, 256), BF16),
            shape((LOC + 1, S, 256), BF16),
            shape((LOC, S, T), F32),
            shape((LOC + 1, S, T), F32),
            shape((8, T), jnp.int32),
            shape((S, 256), BF16),
            shape((S, 256), BF16),
            shape((S, T), F32),
            shape((8, T), F32),
            shape((S, T), F32),
        ),
        in_specs=[hbm] * 10,
        out_specs=(vmem,) * 11,
        scratch_shapes=[
            pltpu.SMEM((LOC,), jnp.int32),
            pltpu.SMEM((LOC,), F32),
            pltpu.SMEM((TOP,), F32),
            pltpu.VMEM((1, TOP), jnp.int32),
            pltpu.VMEM((LEAVES, S, T), F32),
            pltpu.VMEM((S, S), F32),
            pltpu.VMEM((S, S), F32),
            pltpu.VMEM((1, S), F32),
            pltpu.VMEM((S, S), F32),
            pltpu.VMEM((1, S), F32),
            pltpu.VMEM((8, S, T), F32),
            pltpu.SemaphoreType.DMA((10,)),
            pltpu.SemaphoreType.DMA((COPIES,)),
            pltpu.SemaphoreType.DMA((COPIES,)),
        ],
        compiler_params=pltpu.CompilerParams(vmem_limit_bytes=40 << 20, collective_id=0, has_side_effects=True),
        name="prepare",
    )(parents, branch_lengths, top_lengths, top_parents.reshape(1, TOP), tips, eig_vectors, eig_inverse,
      eig_values.reshape(1, S), labeled_rates, root_freq.reshape(1, S))
    w_top, w_loc, m_loc, y_loc, links, eig_w, inv_w, basis, lam, freq = made
    red, _ = pl.pallas_call(
        joining,
        out_shape=(shape((8, T), F32), shape(msg.shape, F32)),
        in_specs=[hbm] * 4 + [smem] + [vmem] * 10,
        out_specs=(vmem, vmem),
        input_output_aliases={5: 1},
        scratch_shapes=[
            pltpu.SMEM((TOP,), jnp.int32),
            pltpu.SMEM((LOC,), jnp.int32),
            pltpu.SMEM((TOP,), F32),
            pltpu.VMEM((1, T), jnp.int32),
            pltpu.SMEM((64,), jnp.int32),
            pltpu.VMEM((72, T), F32),
            pltpu.VMEM((GROUPS, S, T), F32),
            pltpu.VMEM((8, S, T), F32),
            pltpu.VMEM((2, 24, T), F32),
            pltpu.SemaphoreType.DMA((4,)),
        ],
        compiler_params=pltpu.CompilerParams(vmem_limit_bytes=40 << 20),
        name="joining",
    )(top_parents, parents, top_lengths, weights.reshape(1, T), links, msg, w_top, w_loc, m_loc, y_loc,
      eig_w, inv_w, basis, lam, freq)
    ny = lax.axis_size("site")
    count = 2 * ny - 1 + NX * NZ - 1
    out = pl.pallas_call(
        reduce,
        out_shape=shape((8, T), F32),
        in_specs=[vmem],
        out_specs=vmem,
        scratch_shapes=[
            pltpu.VMEM((2 * ny, 8, T), F32),
            pltpu.VMEM((8, T), F32),
            pltpu.VMEM((NX * NZ, 8, T), F32),
            pltpu.SemaphoreType.DMA((count,)),
            pltpu.SemaphoreType.DMA((count,)),
        ],
        compiler_params=pltpu.CompilerParams(collective_id=1, has_side_effects=True),
        name="reduce",
    )(red)
    return out[0, :LOC], out[1, :TOP], out[2]


def solution(mesh):
    placed = (P("leaf", None, "site"), P("leaf"), P("leaf"), P(), P(), P("site"), P(), P(), P(), P(), P())
    return jax.shard_map(
        on_device,
        mesh=mesh,
        in_specs=placed,
        out_specs=(P("leaf"), P(), P("site")),
        check_vma=False,
    )
```

time: 259 us -> 76.3 us (0.29)
  blocking collectives: 112 us -> 0 us
  waiting for transfers between devices: 89.4 us -> 0 us
  Pallas kernels: 24 us -> 63 us
  between operations: 14.1 us -> 0.69 us
  local copies, waits for them, and re-layouts: 16.6 us -> 11.9 us
    psum x2 -> x0, blocking collectives: 112 us -> none  [the longest x1 98.4 us: on_device(): top_sum = lax.psum(out[1], ('leaf', 'site'))]
    all_gather x1 -> x0, waiting for transfers between devices: 89.4 us -> none  [on_device(): gathered = lax.all_gather(sent, 'leaf')]
    pallas_call x2 -> x3, Pallas kernels: 24 us -> 63 us  [the longest x1 34.4 us: on_device(): pl.pallas_call(prepare, out_shape=(shape((ROOT + 1 + WIN, S, T), F32), sh...]
    unnamed x40 -> x24, local copies, waits for them, and re-layouts: 15.4 us -> 8.37 us
    squeeze x2 -> x3, local copies, waits for them, and re-layouts: 0.52 us -> 3.57 us  [on_device(): return (out[0, :LOC], out[1, :TOP], out[2])]
  transfers between devices with their start and end apart: 1 -> 0, of which waited for: 1 -> 0; matrix products, arithmetic and copies ran while one was open for 0% -> 0% of each run, Pallas kernels for 0% -> 0%
where the time goes in v2:
time: 76.3 us; the launch traced here: 75.7 us
  Pallas kernels  63 us (83%)
  local copies, waits for them, and re-layouts  11.9 us (16%)
    pallas_call x1, Pallas kernels, on_device(): pl.pallas_call(prepare, out_shape=(shape((ROOT + 1 + WIN, S, T), F32), sh...  34.4 us
    pallas_call x1, Pallas kernels, on_device(): pl.pallas_call(reduce, out_shape=shape((8, T), F32), in_specs=[vmem], out...  22.3 us
    unnamed x24, local copies, waits for them, and re-layouts  8.37 us
    pallas_call x1, Pallas kernels, on_device(): pl.pallas_call(joining, out_shape=(shape((8, T), F32), shape(msg.shape, F...  6.34 us
    squeeze x3, local copies, waits for them, and re-layouts, on_device(): return (out[0, :LOC], out[1, :TOP], out[2])  3.57 us

profile of v2, /device:TPU:1, one launch (start us, length us, event | category | flops | bytes accessed | tf_op | source)
XLA Modules:
  0.0 75.7 jit_solution(14678506933483287544)
XLA Ops:
  0.6 0.0 copy-start
  0.6 0.9 %copy-done = f32[8,64,128]{2,1,0:T(8,128)S(1)} copy-done((f32[8,64,128]{2,1,0:T(8,128)S(1)}, f32[8,64,128]{2,1,0:T(8,128)}, u32[]{:S(2)}) %copy-start) | copy-done | bytes 262168
  1.6 0.0 copy-start.1
  1.6 0.8 copy-done.1
  2.3 0.0 copy-start.2
  2.3 0.8 copy-done.2
  3.1 0.0 copy-start.3
  3.1 0.8 copy-done.3
  3.9 0.0 copy-start.5
  3.9 0.7 copy-done.5
  4.5 0.0 copy-start.6
  4.5 0.7 copy-done.6
  5.2 0.0 copy-start.7
  5.2 0.7 copy-done.7
  5.8 0.0 copy-start.8
  5.8 0.7 copy-done.8
  6.5 0.0 copy-start.9
  6.5 0.7 copy-done.9
  7.1 0.0 copy-start.10
  7.1 0.7 copy-done.10
  7.8 34.4 %prepare.1 = (f32[131,64,128]{2,1,0:T(8,128)S(1)}, bf16[64,64,256]{2,1,0:T(8,128)(2,1)S(1)}, bf16[15,64,256]{2,1,0:T(8,128)(2,1)S(1)}, f32[14,64,128]{2,1,0:T(8,...) custom-call(s32[14]{0:T(128)S(1)} %copy-done.6, ...), custom_call_target="tpu_custom_call" | custom-call | tf_op jit(solution)/shard_map/prepare/pallas_call | solution.py:500
  42.2 0.0 copy-start.11
  42.3 0.6 copy-done.11
  42.9 6.3 %joining.1 = (f32[8,128]{1,0:T(8,128)S(1)}, f32[131,64,128]{2,1,0:T(8,128)S(1)}) custom-call(s32[126]{0:T(128)S(1)} %copy-done.5, s32[14]{0:T(128)S(1)} %copy-done.6, f32[126]{0:T(128)S(1)} %copy-done.7, s32[1,128]{1,0:T(1,128)S(1)} %bitcast.13, s32[8,128]{1,0:T(8,128)S(1)} %get-tuple-element.15.links, ...), custom_call_target="tpu_custom_call", output_to_operand_aliasing={{1}: (5, {})} | custom-call | tf_op jit(solution)/shard_map/joining/pallas_call | solution.py:538
  49.3 0.0 copy-start.4
  49.3 0.6 copy-done.4
  49.8 22.3 %reduce.1 = f32[8,128]{1,0:T(8,128)} custom-call(f32[8,128]{1,0:T(8,128)} %copy-done.4), custom_call_target="tpu_custom_call" | custom-call | tf_op jit(solution)/shard_map/reduce/pallas_call | solution.py:562
  72.1 1.2 %slice_bitcast_fusion = f32[128]{0:T(128)} fusion(f32[8,128]{1,0:T(8,128)} %reduce.1), kind=kLoop, calls=%fused_computation | loop fusion | bytes 1024 | tf_op jit(solution)/shard_map/squeeze | solution.py:577
  73.3 1.2 %slice_bitcast_fusion.1 = f32[126]{0:T(128)} fusion(f32[8,128]{1,0:T(8,128)} %reduce.1), kind=kLoop, calls=%fused_computation.1 | loop fusion | bytes 1008 | tf_op jit(solution)/shard_map/squeeze | solution.py:577
  74.5 1.2 %slice_bitcast_fusion.2 = f32[14]{0:T(128)} fusion(f32[8,128]{1,0:T(8,128)} %reduce.1), kind=kLoop, calls=%fused_computation.2 | loop fusion | bytes 112 | tf_op jit(solution)/shard_map/squeeze | solution.py:577
Async XLA Ops:
  0.6 1.0 %copy-start = (f32[8,64,128]{2,1,0:T(8,128)S(1)}, f32[8,64,128]{2,1,0:T(8,128)}, u32[]{:S(2)}) copy-start(f32[8,64,128]{2,1,0:T(8,128)} %tips_h.1) | copy-start | bytes 786436
  1.6 0.8 %copy-start.1 = (f32[64,64]{1,0:T(8,128)S(1)}, f32[64,64]{1,0:T(8,128)}, u32[]{:S(2)}) copy-start(f32[64,64]{1,0:T(8,128)} %vectors_h.1) | copy-start | bytes 49156
  2.3 0.8 %copy-start.2 = (f32[64,64]{1,0:T(8,128)S(1)}, f32[64,64]{1,0:T(8,128)}, u32[]{:S(2)}) copy-start(f32[64,64]{1,0:T(8,128)} %inverse_h.1) | copy-start | bytes 49156
  3.1 0.8 %copy-start.3 = (f32[64,64]{1,0:T(8,128)S(1)}, f32[64,64]{1,0:T(8,128)}, u32[]{:S(2)}) copy-start(f32[64,64]{1,0:T(8,128)} %rates_h.1) | copy-start | bytes 49156
  3.9 0.7 copy-start.5
  4.5 0.7 copy-start.6
  5.2 0.7 copy-start.7
  5.8 0.7 copy-start.8
  6.5 0.7 copy-start.9
  7.1 0.7 copy-start.10
  42.2 0.7 copy-start.11
  49.3 0.6 copy-start.4

commit v3 on v2

--- a/solution.py
+++ b/solution.py
@@ -16,12 +16,10 @@
 TOP = 126
 ROOT = 126
 WIN = 4
-NX, NZ, NY = 4, 8, 8
-CUT = 40
-HOPS = ((1, 4), (-1, 3))
 F32 = jnp.float32
 BF16 = jnp.bfloat16
 PRECISE = lax.Precision.HIGHEST
+NX, NZ = 4, 8
 MESH = pl.DeviceIdType.MESH
 
 
@@ -117,7 +115,7 @@
         return ((nx * NZ + nz) * 2 + nc, site)
 
     x_peers = [(dx, 0, 0) for dx in (1, 2, 3)]
-    partners = x_peers + [(0, 1, 0), (0, -1, 0), (0, 0, 1)]
+    partners = x_peers + [(0, dz, 0) for dz in range(1, NZ)] + [(0, 0, 1)]
     barrier = pltpu.get_barrier_semaphore()
     for partner in partners:
         pl.semaphore_signal(barrier, inc=1, device_id=device(*partner), device_id_type=MESH)
@@ -168,13 +166,11 @@
 
     counter = [0]
 
-    def own_piece(xs, zs, rows):
-        if xs is None:
-            return msg.at[pl.ds(slot_of(0, zs, core), NX), rows]
-        return msg.at[slot_of(xs, zs, core), rows]
-
-    def other_piece(zs, rows):
-        return msg.at[pl.ds(slot_of(0, zs, 1 - core), NX), rows]
+    def block(bx, bz, bc):
+        return msg.at[slot_of(bx, bz, bc)]
+
+    def group(bz, bc):
+        return msg.at[pl.ds(slot_of(0, bz, bc), NX)]
 
     started = []
 
@@ -189,28 +185,20 @@
                                                 recv_sem=recv_sem.at[k], device_id=device(*where), device_id_type=MESH)
         return incoming
 
-    first, second = pl.ds(0, CUT), pl.ds(CUT, S - CUT)
-
     def at_z(dz):
         return lax.rem(z + dz + NZ, NZ)
 
     def at_x(dx):
         return lax.rem(x + dx + NX, NX)
 
-    def spread_x(dz):
-        return [send(own_piece(x, at_z(dz), first), (dx, 0, 0), own_piece(at_x(-dx), at_z(dz), first))
-                for dx in (1, 2, 3)]
-
-    def cross(dz, rows):
-        return send(own_piece(None, at_z(dz), rows), (0, 0, 1), other_piece(at_z(dz), rows))
-
-    def hop_first(direction, h):
-        return send(own_piece(x, at_z(-direction * (h - 1)), first), (0, direction, 0),
-                    own_piece(x, at_z(-direction * h), first))
-
-    def hop_second(direction, h):
-        return send(own_piece(None, at_z(-direction * (h - 1)), second), (0, direction, 0),
-                    own_piece(None, at_z(-direction * h), second))
+    def along_z(dz):
+        return send(block(x, z, core), (0, dz, 0), block(x, at_z(-dz), core))
+
+    def along_x(dz):
+        return [send(block(x, at_z(-dz), core), (dx, 0, 0), block(at_x(-dx), at_z(-dz), core)) for dx in (1, 3, 2)]
+
+    def across(dz):
+        return send(group(at_z(-dz), core), (0, 0, 1), group(at_z(-dz), 1 - core))
 
     def work(stage):
         if stage == 0:
@@ -248,57 +236,40 @@
 
             lax.fori_loop(lo, hi, some, 0)
 
-    x_second = [send(own_piece(x, z, second), (dx, 0, 0), own_piece(at_x(-dx), z, second)) for dx in (1, 2, 3)]
-    z_first = {d: hop_first(d, 1) for d, _ in HOPS}
-    spreads = [(0, spread_x(0))]
+    order = (1, -1, 2, -2, 3, -3, 4)
+    from_x = {0: along_x(0)}
+    from_z = {dz: along_z(dz) for dz in order}
     crossed = []
+
+    def close(dz):
+        for one in from_x[dz]:
+            one.wait_recv()
+        crossed.append(across(dz))
+
     work(0)
-    for incoming in x_second:
-        incoming.wait_recv()
-    z_second = {d: hop_second(d, 1) for d, _ in HOPS}
-    crossed.append(cross(0, second))
-    for h in range(1, 5):
-        work(h)
-        for d, most in HOPS:
-            if h > most:
-                continue
-            z_first[d].wait_recv()
-            if h < most:
-                z_first[d] = hop_first(d, h + 1)
-            spreads.append((-d * h, spread_x(-d * h)))
-        for d, most in HOPS:
-            if h > most:
-                continue
-            z_second[d].wait_recv()
-            if h < most:
-                z_second[d] = hop_second(d, h + 1)
-            crossed.append(cross(-d * h, second))
-        ready, spreads = spreads[:-2], spreads[-2:]
-        for dz, incoming in ready:
-            for one in incoming:
-                one.wait_recv()
-            crossed.append(cross(dz, first))
-    work(5)
-    for dz, incoming in spreads:
-        for one in incoming:
-            one.wait_recv()
-        crossed.append(cross(dz, first))
-    work(6)
+    for i, dz in enumerate(order):
+        from_z[dz].wait_recv()
+        from_x[dz] = along_x(dz)
+        if i >= 1:
+            close(((0,) + order)[i - 1])
+        if i < 6:
+            work(i + 1)
+    for dz in order[-2:]:
+        close(dz)
     for one in crossed:
         one.wait_recv()
     for one in started:
         one.wait_send()
 
 
-COPIES = 3 + 7 + 24 + 7 + 16
-
-
-def joining(top_parents_h, parents_h, top_lengths_h, weights_h, links, msg_in, w_top, w_loc, m_loc, y_loc,
-            eig_w, inv_w, basis, lam, freq, out, msg,
-            top_parents, parents, top_lengths, weights, path, factor, arrs, o_loc, rows, sem):
+COPIES = (NZ - 1) + 3 * NZ + NZ
+
+
+def joining(top_parents_h, top_lengths_h, links, msg_in, w_top, freq, loglik, handed, info, msg,
+            top_parents, top_lengths, path, factor, arrs, sem):
     del msg_in
     loads = [pltpu.make_async_copy(src, dst, sem.at[i]) for i, (src, dst) in enumerate((
-        (top_parents_h, top_parents), (parents_h, parents), (top_lengths_h, top_lengths), (weights_h, weights)))]
+        (top_parents_h, top_parents), (top_lengths_h, top_lengths)))]
     for load in loads:
         load.start()
     me = lax.axis_index("leaf")
@@ -340,7 +311,7 @@
     likelihood = jnp.sum(freq_col * root_u, axis=0, keepdims=True)
     row = iota((72, T), 0)
     top_logs = -jnp.sum(jnp.log(jnp.where(row < TOP - GROUPS, factor[...], 1.0)), axis=0, keepdims=True)
-    loglik = (jnp.log(likelihood) + top_logs + local_logs) * (1.0 / (GROUPS * LEAVES))
+    loglik[...] = (jnp.log(likelihood) + top_logs + local_logs) * (1.0 / (GROUPS * LEAVES))
     for load in loads:
         load.wait()
 
@@ -367,24 +338,67 @@
 
     o = lax.fori_loop(0, depth - 1, step_down, jnp.ones((S, T), F32))
     p = top_parents[me]
-    arriving = o * msg[late(p) + early(p) - slot]
-    arrs[0] = arriving
-    o_loc[LOC - LEAVES] = apply(w_loc[LOC], arriving) * inverse(biggest(arriving))
-
-    def ratio(place, arriving, message, y):
+    leaf_arriving = o * msg[late(p) + early(p) - slot]
+    arrs[0] = leaf_arriving
+    handed[0] = leaf_arriving
+    handed[1] = msg[slot]
+    handed[2] = arrs[at]
+    handed[3] = msg[node]
+    handed[4] = msg[late(node)] * msg[early(node)] * factor[pl.ds(node - GROUPS, 1)]
+    row = iota((8, T), 0)
+    info[...] = jnp.where(row == 0, top_lengths[node], jnp.where(counted, node, -1).astype(F32))
+
+
+PHASES = ("y", "c", "x", "z")
+
+
+def tail(parents_h, weights_h, handed, info, w_loc, m_loc, y_loc, eig_w, inv_w, basis, lam, freq, local_out, top_out,
+         parents, weights, o_loc, rows, *rest):
+    bufs, parts = rest[:len(PHASES)], rest[len(PHASES):2 * len(PHASES)]
+    in_sem, send_sem, recv_sem = rest[2 * len(PHASES):]
+    loads = [pltpu.make_async_copy(parents_h, parents, in_sem.at[0]), pltpu.make_async_copy(weights_h, weights, in_sem.at[1])]
+    for load in loads:
+        load.start()
+    me = lax.axis_index("leaf")
+    sizes = {"x": NX, "z": NZ, "c": 2, "y": lax.axis_size("site")}
+    here = {"x": me // (2 * NZ), "z": lax.rem(me // 2, NZ), "c": lax.rem(me, 2), "y": lax.axis_index("site")}
+
+    def shifted(offset):
+        return {a: (lax.rem(here[a] + offset.get(a, 0) + sizes[a], sizes[a])) for a in here}
+
+    def device(offset):
+        at = shifted(offset)
+        return ((at["x"] * NZ + at["z"]) * 2 + at["c"], at["y"])
+
+    def place(axes, at):
+        index = 0
+        for a in axes:
+            index = index * sizes[a] + at[a]
+        return index
+
+    offsets = [phase_offsets(axes, sizes) for axes in PHASES]
+    barrier = pltpu.get_barrier_semaphore()
+    for some in offsets:
+        for offset in some:
+            pl.semaphore_signal(barrier, inc=1, device_id=device(offset), device_id_type=MESH)
+
+    freq_col = freq[...]
+
+    def ratio(row, arriving, message, y):
         weighted = freq_col * arriving
-        rows[0, pl.ds(place, 1)] = jnp.sum(weighted * y, axis=0, keepdims=True)
-        rows[1, pl.ds(place, 1)] = jnp.sum(weighted * message, axis=0, keepdims=True)
+        rows[0, pl.ds(row, 1)] = jnp.sum(weighted * y, axis=0, keepdims=True)
+        rows[1, pl.ds(row, 1)] = jnp.sum(weighted * message, axis=0, keepdims=True)
 
     rows[...] = jnp.ones((2, 24, T), F32)
-    ratio(16, arriving, msg[slot], y_loc[LOC])
     lam2 = lam[0:1]
-    v = apply(inv_w[...], msg[late(node)] * msg[early(node)]) * factor[pl.ds(node - GROUPS, 1)]
-    y = apply(eig_w[...], apply(held_integrals(basis[...], lam2, column(lam2[:, :S]), top_lengths[node]), v))
-    ratio(17, arrs[at], msg[node], y)
-
+    o_loc[LOC - LEAVES] = apply(w_loc[LOC], handed[0]) * inverse(biggest(handed[0]))
+    ratio(16, handed[0], handed[1], y_loc[LOC])
+    held = held_integrals(basis[...], lam2, column(lam2[:, :S]), info[0:1, 0:1])
+    ratio(17, handed[2], handed[3], apply(eig_w[...], apply(held, apply(inv_w[...], handed[4]))))
+    for load in loads:
+        load.wait()
     for c in range(LOC - 1, -1, -1):
-        p = parents[c]
+        p = jnp.clip(parents[c], LEAVES, LOC)
         sibling = jnp.int32(0)
         for other in range(LOC):
             if other != c:
@@ -393,107 +407,59 @@
         if c >= LEAVES:
             o_loc[c - LEAVES] = apply(w_loc[c], arriving) * inverse(biggest(arriving))
         ratio(c, arriving, m_loc[c], y_loc[c])
-
     weight = weights[...].astype(F32)
-    expected = weight * rows[0] / rows[1]
-    place = iota((24, T), 0)
-    expected = jnp.where(place == LOC, weight, expected)
+    expected = jnp.where(iota((24, T), 0) == LOC, weight, weight * rows[0] / rows[1])
     sums = lax.dot_general(jnp.ones((8, T), F32), expected, (((1,), (1,)), ((), ())),
                            precision=PRECISE, preferred_element_type=F32)
     lane = iota((1, T), 1)
-    own = sums[0:1, 16:17]
-    inner = sums[0:1, 17:18]
-    top_row = jnp.where(lane == me, own, 0.0) + jnp.where((lane == node) & counted, inner, 0.0)
-    out[...] = jnp.zeros((8, T), F32)
-    out[pl.ds(0, 1), pl.ds(0, 24)] = sums[0:1]
-    out[pl.ds(1, 1)] = top_row
-    out[pl.ds(2, 1)] = loglik
-
-
-def reduce(mine, out, near, partial, far, send_sem, recv_sem):
-    me = lax.axis_index("leaf")
-    y = lax.axis_index("site")
-    ny = lax.axis_size("site")
-    core = lax.rem(me, 2)
-    z = lax.rem(me // 2, NZ)
-    x = me // (2 * NZ)
-    nears = [(dy, dc) for dy in range(ny) for dc in (0, 1) if (dy, dc) != (0, 0)]
-    fars = [(dx, dz) for dx in range(NX) for dz in range(NZ) if (dx, dz) != (0, 0)]
-
-    def near_at(dy, dc):
-        return lax.rem(y + dy + ny, ny), (1 - core if dc else core)
-
-    def far_at(dx, dz):
-        return lax.rem(x + dx + NX, NX), lax.rem(z + dz + NZ, NZ)
-
-    def near_device(dy, dc):
-        ty, tc = near_at(dy, dc)
-        return ((x * NZ + z) * 2 + tc, ty)
-
-    def far_device(dx, dz):
-        tx, tz = far_at(dx, dz)
-        return ((tx * NZ + tz) * 2 + core, y)
-
-    barrier = pltpu.get_barrier_semaphore()
-    for where in nears:
-        pl.semaphore_signal(barrier, inc=1, device_id=near_device(*where), device_id_type=MESH)
-    for where in fars:
-        pl.semaphore_signal(barrier, inc=1, device_id=far_device(*where), device_id_type=MESH)
-    pl.semaphore_wait(barrier, len(nears) + len(fars))
-
-    def near_slot(ty, tc):
-        return ty * 2 + tc
-
-    near[near_slot(y, core)] = mine[...]
+    node = info[1:2]
+    top_row = jnp.where(lane == me, sums[0:1, 16:17], 0.0) + jnp.where(lane.astype(F32) == node, sums[0:1, 17:18], 0.0)
+    parts[0][...] = jnp.zeros((8, T), F32)
+    parts[0][pl.ds(0, 1), pl.ds(0, 24)] = sums[0:1]
+    parts[0][pl.ds(1, 1)] = top_row
+    pl.semaphore_wait(barrier, sum(map(len, offsets)))
+
+    k = 0
     copies = []
-    arrivals = []
-    for k, (dy, dc) in enumerate(nears):
-        here = near.at[near_slot(y, core)]
-        copy = pltpu.make_async_remote_copy(src_ref=mine, dst_ref=here, send_sem=send_sem.at[k],
-                                            recv_sem=recv_sem.at[k], device_id=near_device(dy, dc), device_id_type=MESH)
-        copy.start()
-        copies.append(copy)
-        there = near.at[near_slot(*near_at(-dy, dc))]
-        arrivals.append(pltpu.make_async_remote_copy(
-            src_ref=there, dst_ref=there, send_sem=send_sem.at[k], recv_sem=recv_sem.at[k],
-            device_id=near_device(dy, dc), device_id_type=MESH))
-    for arrival in arrivals:
-        arrival.wait_recv()
-    local = near[core]
-    top = near[0] + near[1]
-    for i in range(1, ny):
-        local = local + near[2 * i + core]
-        top = top + (near[2 * i] + near[2 * i + 1])
-    partial[...] = top
-    far[x * NZ + z] = top
-    base = len(nears)
-    arrivals = []
-    for k, (dx, dz) in enumerate(fars):
-        copy = pltpu.make_async_remote_copy(src_ref=partial, dst_ref=far.at[x * NZ + z], send_sem=send_sem.at[base + k],
-                                            recv_sem=recv_sem.at[base + k], device_id=far_device(dx, dz), device_id_type=MESH)
-        copy.start()
-        copies.append(copy)
-        tx, tz = far_at(-dx, -dz)
-        there = far.at[tx * NZ + tz]
-        arrivals.append(pltpu.make_async_remote_copy(
-            src_ref=there, dst_ref=there, send_sem=send_sem.at[base + k], recv_sem=recv_sem.at[base + k],
-            device_id=far_device(dx, dz), device_id_type=MESH))
-    for arrival in arrivals:
-        arrival.wait_recv()
-    top = far[0]
-    for i in range(1, NX * NZ):
-        top = top + far[i]
-    total = local[0:1, LOC:LOC + 1]
-    out[...] = mine[...]
-    out[pl.ds(0, 1)] = local[0:1] / total
-    out[pl.ds(1, 1)] = top[1:2] / total
+    for i, (axes, some) in enumerate(zip(PHASES, offsets)):
+        buf, part = bufs[i], parts[i]
+        mine = place(axes, here)
+        buf[mine] = part[...]
+        arrivals = []
+        for offset in some:
+            copy = pltpu.make_async_remote_copy(src_ref=part, dst_ref=buf.at[mine], send_sem=send_sem.at[k],
+                                                recv_sem=recv_sem.at[k], device_id=device(offset), device_id_type=MESH)
+            copy.start()
+            copies.append(copy)
+            there = buf.at[place(axes, shifted({a: -n for a, n in offset.items()}))]
+            arrivals.append(pltpu.make_async_remote_copy(
+                src_ref=there, dst_ref=there, send_sem=send_sem.at[k], recv_sem=recv_sem.at[k],
+                device_id=device(offset), device_id_type=MESH))
+            k += 1
+        for arrival in arrivals:
+            arrival.wait_recv()
+        total = jnp.sum(buf[...], axis=0)
+        if i == 0:
+            weight_total = total[0:1, LOC:LOC + 1]
+            local_out[...] = (total[0:1] / weight_total)[:, :LOC]
+        if i + 1 < len(PHASES):
+            parts[i + 1][...] = total
+    top_out[...] = (total[1:2] / weight_total)[:, :TOP]
     for copy in copies:
         copy.wait_send()
+
+
+def phase_offsets(axes, sizes):
+    found = [{}]
+    for a in axes:
+        found = [{**one, a: n} for one in found for n in range(sizes[a])]
+    return [one for one in found if any(one.values())]
 
 
 def on_device(tips, parents, branch_lengths, top_parents, top_lengths, weights, eig_vectors,
               eig_inverse, eig_values, labeled_rates, root_freq):
     hbm = pl.BlockSpec(memory_space=pltpu.HBM)
+    stay = functools.partial(pltpu.with_memory_space_constraint, memory_space=pltpu.HBM)
     smem = pl.BlockSpec(memory_space=pltpu.SMEM)
     vmem = pl.BlockSpec(memory_space=pltpu.VMEM)
     shape = jax.ShapeDtypeStruct
@@ -532,49 +498,48 @@
         ],
         compiler_params=pltpu.CompilerParams(vmem_limit_bytes=40 << 20, collective_id=0, has_side_effects=True),
         name="prepare",
-    )(parents, branch_lengths, top_lengths, top_parents.reshape(1, TOP), tips, eig_vectors, eig_inverse,
-      eig_values.reshape(1, S), labeled_rates, root_freq.reshape(1, S))
+    )(*map(stay, (parents, branch_lengths, top_lengths, top_parents.reshape(1, TOP), tips, eig_vectors, eig_inverse,
+                   eig_values.reshape(1, S), labeled_rates, root_freq.reshape(1, S))))
     w_top, w_loc, m_loc, y_loc, links, eig_w, inv_w, basis, lam, freq = made
-    red, _ = pl.pallas_call(
+    loglik, handed, info, _ = pl.pallas_call(
         joining,
-        out_shape=(shape((8, T), F32), shape(msg.shape, F32)),
-        in_specs=[hbm] * 4 + [smem] + [vmem] * 10,
-        out_specs=(vmem, vmem),
-        input_output_aliases={5: 1},
+        out_shape=(shape((1, T), F32), shape((5, S, T), F32), shape((8, T), F32), shape(msg.shape, F32)),
+        in_specs=[hbm] * 2 + [smem] + [vmem] * 3,
+        out_specs=(vmem,) * 4,
+        input_output_aliases={3: 3},
         scratch_shapes=[
             pltpu.SMEM((TOP,), jnp.int32),
-            pltpu.SMEM((LOC,), jnp.int32),
             pltpu.SMEM((TOP,), F32),
-            pltpu.VMEM((1, T), jnp.int32),
             pltpu.SMEM((64,), jnp.int32),
             pltpu.VMEM((72, T), F32),
             pltpu.VMEM((GROUPS, S, T), F32),
+            pltpu.SemaphoreType.DMA((2,)),
+        ],
+        compiler_params=pltpu.CompilerParams(vmem_limit_bytes=24 << 20),
+        name="joining",
+    )(*map(stay, (top_parents, top_lengths)), links, msg, w_top, freq)
+    sizes = {"x": NX, "z": NZ, "c": 2, "y": lax.axis_size("site")}
+    offsets = [phase_offsets(axes, sizes) for axes in PHASES]
+    count = sum(map(len, offsets))
+    local, top = pl.pallas_call(
+        tail,
+        out_shape=(shape((1, LOC), F32), shape((1, TOP), F32)),
+        in_specs=[hbm] * 2 + [vmem] * 10,
+        out_specs=(vmem, vmem),
+        scratch_shapes=[
+            pltpu.SMEM((LOC,), jnp.int32),
+            pltpu.VMEM((1, T), jnp.int32),
             pltpu.VMEM((8, S, T), F32),
             pltpu.VMEM((2, 24, T), F32),
-            pltpu.SemaphoreType.DMA((4,)),
-        ],
-        compiler_params=pltpu.CompilerParams(vmem_limit_bytes=40 << 20),
-        name="joining",
-    )(top_parents, parents, top_lengths, weights.reshape(1, T), links, msg, w_top, w_loc, m_loc, y_loc,
-      eig_w, inv_w, basis, lam, freq)
-    ny = lax.axis_size("site")
-    count = 2 * ny - 1 + NX * NZ - 1
-    out = pl.pallas_call(
-        reduce,
-        out_shape=shape((8, T), F32),
-        in_specs=[vmem],
-        out_specs=vmem,
-        scratch_shapes=[
-            pltpu.VMEM((2 * ny, 8, T), F32),
-            pltpu.VMEM((8, T), F32),
-            pltpu.VMEM((NX * NZ, 8, T), F32),
+        ] + [pltpu.VMEM((len(some) + 1, 8, T), F32) for some in offsets] + [pltpu.VMEM((8, T), F32) for _ in offsets] + [
+            pltpu.SemaphoreType.DMA((2,)),
             pltpu.SemaphoreType.DMA((count,)),
             pltpu.SemaphoreType.DMA((count,)),
         ],
-        compiler_params=pltpu.CompilerParams(collective_id=1, has_side_effects=True),
-        name="reduce",
-    )(red)
-    return out[0, :LOC], out[1, :TOP], out[2]
+        compiler_params=pltpu.CompilerParams(vmem_limit_bytes=24 << 20, collective_id=1, has_side_effects=True),
+        name="tail",
+    )(*map(stay, (parents, weights.reshape(1, T))), handed, info, w_loc, m_loc, y_loc, eig_w, inv_w, basis, lam, freq)
+    return local.reshape(LOC), top.reshape(TOP), loglik.reshape(T)
 
 
 def solution(mesh):

time: 76.3 us -> 60.3 us (0.79)
  local copies, waits for them, and re-layouts: 11.9 us -> 1.02 us
  Pallas kernels: 63 us -> 58.5 us
    unnamed x24 -> x2, local copies, waits for them, and re-layouts: 8.37 us -> 1.02 us
    pallas_call x2, Pallas kernels: 28.6 us -> 24.6 us  [the longest x1 18.8 us: on_device(): pl.pallas_call(tail, out_shape=(shape((1, LOC), F32), shape((1, TOP), F32...]
    squeeze x3 -> x0, local copies, waits for them, and re-layouts: 3.57 us -> none  [on_device(): return (out[0, :LOC], out[1, :TOP], out[2])]
where the time goes in v3:
time: 60.3 us; the launch traced here: 60.2 us
  Pallas kernels  58.5 us (97%)
  local copies, waits for them, and re-layouts  1.02 us (2%)
  between operations  0.66 us (1%)
    pallas_call x1, Pallas kernels, on_device(): pl.pallas_call(prepare, out_shape=(shape((ROOT + 1 + WIN, S, T), F32), sh...  33.9 us
    pallas_call x1, Pallas kernels, on_device(): pl.pallas_call(tail, out_shape=(shape((1, LOC), F32), shape((1, TOP), F32...  18.8 us
    pallas_call x1, Pallas kernels, on_device(): pl.pallas_call(joining, out_shape=(shape((1, T), F32), shape((5, S, T), F...  5.75 us

profile of v3, /device:TPU:1, one launch (start us, length us, event | category | flops | bytes accessed | tf_op | source)
XLA Modules:
  0.0 60.2 jit_solution(7379851448254383561)
XLA Ops:
  0.6 33.9 %prepare.1 = (f32[131,64,128]{2,1,0:T(8,128)S(1)}, bf16[64,64,256]{2,1,0:T(8,128)(2,1)S(1)}, bf16[15,64,256]{2,1,0:T(8,128)(2,1)S(1)}, f32[14,64,128]{2,1,0:T(8,...) custom-call(s32[14]{0:T(128)} %parents_h.3, ...), custom_call_target="tpu_custom_call" | custom-call | tf_op jit(solution)/shard_map/prepare/pallas_call | solution.py:466
  34.6 5.7 %joining.1 = (f32[1,128]{1,0:T(1,128)}, f32[5,64,128]{2,1,0:T(8,128)S(1)}, f32[8,128]{1,0:T(8,128)S(1)}, f32[131,64,128]{2,1,0:T(8,128)S(1)}) custom-call(s32[126]{0:T(128)} %top_parents_h.1, f32[126]{0:T(128)} %top_lengths_h.3, s32[8,128]{1,0:T(8,128)S(1)} %get-tuple-element.19.links, ...), custom_call_target="tpu_custom_call", output_to_operand_aliasing={{3}: (3, {})} | custom-call | tf_op jit(solution)/shard_map/joining/pallas_call | solution.py:504
  40.3 18.8 %tail.1 = (f32[1,14]{1,0:T(1,128)S(1)}, f32[1,126]{1,0:T(1,128)S(1)}) custom-call(s32[14]{0:T(128)} %parents_h.3, s32[1,128]{1,0:T(1,128)} %bitcast.12, f32[5,64,128]{2,1,0:T(8,128)S(1)} %get-tuple-element.23.handed, f32[8,128]{1,0:T(8,128)S(1)} %get-tuple-element.24.info, bf16[15,64,256]{2,1,0:T(8,128)(2,1)S(1)} %get-tuple-element.25.w_loc, ...), custom_call_target="tpu_custom_call" | custom-call | tf_op jit(solution)/shard_map/tail/pallas_call | solution.py:524
  59.1 0.5 copy.18
  59.6 0.5 copy.19

commit v4 on v3

--- a/solution.py
+++ b/solution.py
@@ -15,7 +15,8 @@
 GROUPS = 64
 TOP = 126
 ROOT = 126
-WIN = 4
+WIN = 6
+ACROSS = 16
 F32 = jnp.float32
 BF16 = jnp.bfloat16
 PRECISE = lax.Precision.HIGHEST
@@ -166,11 +167,13 @@
 
     counter = [0]
 
-    def block(bx, bz, bc):
-        return msg.at[slot_of(bx, bz, bc)]
-
-    def group(bz, bc):
-        return msg.at[pl.ds(slot_of(0, bz, bc), NX)]
+    main, rest = pl.ds(0, S - ACROSS), pl.ds(S - ACROSS, ACROSS)
+
+    def block(bx, bz, bc, rows):
+        return msg.at[slot_of(bx, bz, bc), rows]
+
+    def group(bz, bc, rows):
+        return msg.at[pl.ds(slot_of(0, bz, bc), NX), rows]
 
     started = []
 
@@ -192,77 +195,103 @@
         return lax.rem(x + dx + NX, NX)
 
     def along_z(dz):
-        return send(block(x, z, core), (0, dz, 0), block(x, at_z(-dz), core))
-
-    def along_x(dz):
-        return [send(block(x, at_z(-dz), core), (dx, 0, 0), block(at_x(-dx), at_z(-dz), core)) for dx in (1, 3, 2)]
-
-    def across(dz):
-        return send(group(at_z(-dz), core), (0, 0, 1), group(at_z(-dz), 1 - core))
-
-    def work(stage):
-        if stage == 0:
-            loads[7].wait()
-            loads[8].wait()
-            loads[9].wait()
-            parent_col = column(top_parents[...])
-            child = iota((TOP, T), 0)
-            hit = parent_col == iota((TOP, T), 1)
-            late = jnp.max(jnp.where(hit, child, 0), axis=0, keepdims=True)
-            early = jnp.min(jnp.where(hit, child, TOP), axis=0, keepdims=True)
-            pair = jnp.concatenate([late, early, jnp.zeros((6, T), jnp.int32)], axis=0)
-            slots = (pair & 1) * (NX * NZ) + ((pair >> 1) & (NZ - 1)) * NX + (pair >> 4)
-            pair = jnp.where(pair < GROUPS, slots, pair)
-            lane = iota((8, T), 1)
-            links[...] = jnp.where((lane >= GROUPS) & (lane <= ROOT), pair, 0)
-            freq_out[...] = jnp.broadcast_to(column(freq[...]), (S, T))
-            lam_out[...] = jnp.broadcast_to(lam2, (8, T))
-            basis_out[...] = double(dot(dot(left, rates[...]), right))
-            eig_w[...] = pack(right2)
-            inv_w[...] = pack(double(left))
-        elif stage <= 4:
-            per = 4
-            for c in range((stage - 1) * per, min(stage * per, LOC + 1)):
-                t = lengths[c] if c < LOC else top_lengths[me]
-                v = apply(inv_w[...], tips[c] if c < LEAVES else x_int[c - LEAVES])
-                y_loc[c] = apply(eig_w[...], apply(held_integrals(basis_out[...], lam2, lam_col, t), v))
-        else:
-            lo, hi = ((0, 4), (4, 8))[stage - 5]
-
-            def some(i, _):
-                for j, w in enumerate(branches([top_lengths[jnp.minimum(GROUPS + i * 8 + j, TOP - 1)] for j in range(8)])):
-                    w_top[i * 8 + j] = w
-                return 0
-
-            lax.fori_loop(lo, hi, some, 0)
+        return send(block(x, z, core, main), (0, dz, 0), block(x, at_z(-dz), core, main))
+
+    def along_x(dz, rows):
+        return [send(block(x, at_z(-dz), core, rows), (dx, 0, 0), block(at_x(-dx), at_z(-dz), core, rows))
+                for dx in (1, 3, 2)]
+
+    def group_z(dz):
+        return send(group(z, core, rest), (0, dz, 0), group(at_z(-dz), core, rest))
+
+    def across(dz, rows):
+        return send(group(at_z(-dz), core, rows), (0, 0, 1), group(at_z(-dz), 1 - core, rows))
+
+    def shared():
+        loads[7].wait()
+        loads[8].wait()
+        loads[9].wait()
+        parent_col = column(top_parents[...])
+        child = iota((TOP, T), 0)
+        hit = parent_col == iota((TOP, T), 1)
+        late = jnp.max(jnp.where(hit, child, 0), axis=0, keepdims=True)
+        early = jnp.min(jnp.where(hit, child, TOP), axis=0, keepdims=True)
+        pair = jnp.concatenate([late, early, jnp.zeros((6, T), jnp.int32)], axis=0)
+        slots = (pair & 1) * (NX * NZ) + ((pair >> 1) & (NZ - 1)) * NX + (pair >> 4)
+        pair = jnp.where(pair < GROUPS, slots, pair)
+        lane = iota((8, T), 1)
+        links[...] = jnp.where((lane >= GROUPS) & (lane <= ROOT), pair, 0)
+        freq_out[...] = jnp.broadcast_to(column(freq[...]), (S, T))
+        lam_out[...] = jnp.broadcast_to(lam2, (8, T))
+        basis_out[...] = double(dot(dot(left, rates[...]), right))
+        eig_w[...] = pack(right2)
+        inv_w[...] = pack(double(left))
+
+    def products(lo, hi):
+        for c in range(lo, hi):
+            t = lengths[c] if c < LOC else top_lengths[me]
+            v = apply(inv_w[...], tips[c] if c < LEAVES else x_int[c - LEAVES])
+            y_loc[c] = apply(eig_w[...], apply(held_integrals(basis_out[...], lam2, lam_col, t), v))
+
+    def matrices(lo, hi):
+        def some(i, _):
+            ts = [top_lengths[jnp.minimum(GROUPS + i * 8 + j, TOP - 1)] for j in range(8)]
+            for j, w in enumerate(branches(ts)):
+                w_top[i * 8 + j] = w
+            return 0
+
+        lax.fori_loop(lo, hi, some, 0)
 
     order = (1, -1, 2, -2, 3, -3, 4)
-    from_x = {0: along_x(0)}
-    from_z = {dz: along_z(dz) for dz in order}
+    turns = (0,) + order
+    first = along_x(0, rest)
+    from_z = {dz: along_z(dz) for dz in order[:2]}
+    from_x = {0: along_x(0, main)}
+    from_z.update({dz: along_z(dz) for dz in order[2:]})
     crossed = []
-
-    def close(dz):
+    closed = [0]
+
+    def close():
+        dz = turns[closed[0]]
+        closed[0] += 1
         for one in from_x[dz]:
             one.wait_recv()
-        crossed.append(across(dz))
-
-    work(0)
+        crossed.append(across(dz, main))
+
+    shared()
     for i, dz in enumerate(order):
         from_z[dz].wait_recv()
-        from_x[dz] = along_x(dz)
-        if i >= 1:
-            close(((0,) + order)[i - 1])
-        if i < 6:
-            work(i + 1)
-    for dz in order[-2:]:
-        close(dz)
+        from_x[dz] = along_x(dz, main)
+        if i == 0:
+            for one in first:
+                one.wait_recv()
+            groups = {d: group_z(d) for d in order}
+            crossed.append(across(0, rest))
+        if i >= 5:
+            close()
+        if i in (1, 3, 5):
+            matrices(i - 1, i + 1)
+    products(0, 5)
+    for i, dz in enumerate(order):
+        groups[dz].wait_recv()
+        crossed.append(across(dz, rest))
+        if closed[0] < len(turns):
+            close()
+        if i == 1:
+            products(5, 10)
+        if i == 3:
+            products(10, 15)
+        if i == 5:
+            matrices(6, 8)
+    while closed[0] < len(turns):
+        close()
     for one in crossed:
         one.wait_recv()
     for one in started:
         one.wait_send()
 
 
-COPIES = (NZ - 1) + 3 * NZ + NZ
+COPIES = 3 * (NZ + 1) + 2 * (NZ - 1) + 2 * NZ
 
 
 def joining(top_parents_h, top_lengths_h, links, msg_in, w_top, freq, loglik, handed, info, msg,
@@ -349,7 +378,7 @@
     info[...] = jnp.where(row == 0, top_lengths[node], jnp.where(counted, node, -1).astype(F32))
 
 
-PHASES = ("y", "c", "x", "z")
+PHASES = ("yc", "x", "z")
 
 
 def tail(parents_h, weights_h, handed, info, w_loc, m_loc, y_loc, eig_w, inv_w, basis, lam, freq, local_out, top_out,
@@ -409,14 +438,13 @@
         ratio(c, arriving, m_loc[c], y_loc[c])
     weight = weights[...].astype(F32)
     expected = jnp.where(iota((24, T), 0) == LOC, weight, weight * rows[0] / rows[1])
+    expected = jnp.concatenate([expected, jnp.zeros((T - 24, T), F32)], axis=0)
     sums = lax.dot_general(jnp.ones((8, T), F32), expected, (((1,), (1,)), ((), ())),
                            precision=PRECISE, preferred_element_type=F32)
     lane = iota((1, T), 1)
     node = info[1:2]
     top_row = jnp.where(lane == me, sums[0:1, 16:17], 0.0) + jnp.where(lane.astype(F32) == node, sums[0:1, 17:18], 0.0)
-    parts[0][...] = jnp.zeros((8, T), F32)
-    parts[0][pl.ds(0, 1), pl.ds(0, 24)] = sums[0:1]
-    parts[0][pl.ds(1, 1)] = top_row
+    parts[0][...] = jnp.concatenate([sums[0:1], top_row], axis=0)
     pl.semaphore_wait(barrier, sum(map(len, offsets)))
 
     k = 0
@@ -438,13 +466,21 @@
             k += 1
         for arrival in arrivals:
             arrival.wait_recv()
-        total = jnp.sum(buf[...], axis=0)
         if i == 0:
-            weight_total = total[0:1, LOC:LOC + 1]
-            local_out[...] = (total[0:1] / weight_total)[:, :LOC]
+            local = buf[here["c"], 0:1]
+            total = buf[0, 1:2] + buf[1, 1:2]
+            for n in range(1, sizes["y"]):
+                local = local + buf[2 * n + here["c"], 0:1]
+                total = total + (buf[2 * n, 1:2] + buf[2 * n + 1, 1:2])
+            weight_total = local[:, LOC:LOC + 1]
+            local_out[...] = (local / weight_total)[:, :LOC]
+        else:
+            total = buf[0]
+            for n in range(1, len(some) + 1):
+                total = total + buf[n]
         if i + 1 < len(PHASES):
             parts[i + 1][...] = total
-    top_out[...] = (total[1:2] / weight_total)[:, :TOP]
+    top_out[...] = (total / weight_total)[:, :TOP]
     for copy in copies:
         copy.wait_send()
 
@@ -531,7 +567,8 @@
             pltpu.VMEM((1, T), jnp.int32),
             pltpu.VMEM((8, S, T), F32),
             pltpu.VMEM((2, 24, T), F32),
-        ] + [pltpu.VMEM((len(some) + 1, 8, T), F32) for some in offsets] + [pltpu.VMEM((8, T), F32) for _ in offsets] + [
+        ] + [pltpu.VMEM((len(some) + 1, 1 if i else 2, T), F32) for i, some in enumerate(offsets)] + [
+            pltpu.VMEM((1 if i else 2, T), F32) for i in range(len(offsets))] + [
             pltpu.SemaphoreType.DMA((2,)),
             pltpu.SemaphoreType.DMA((count,)),
             pltpu.SemaphoreType.DMA((count,)),

time: 60.3 us -> 54.1 us (0.90); the launches traced: 60.2 us -> 53.3 us
  Pallas kernels: 58.5 us -> 51.7 us
    pallas_call x1, Pallas kernels: 33.9 us -> 29.1 us  [on_device(): pl.pallas_call(prepare, out_shape=(shape((ROOT + 1 + WIN, S, T), F32), sh...]
    pallas_call x1, Pallas kernels: 18.8 us -> 16.7 us  [on_device(): pl.pallas_call(tail, out_shape=(shape((1, LOC), F32), shape((1, TOP), F32...]
where the time goes in v4:
time: 54.1 us; the launch traced here: 53.3 us
  Pallas kernels  51.7 us (96%)
  local copies, waits for them, and re-layouts  1.02 us (2%)
  between operations  0.66 us (1%)
    pallas_call x1, Pallas kernels, on_device(): pl.pallas_call(prepare, out_shape=(shape((ROOT + 1 + WIN, S, T), F32), sh...  29.1 us
    pallas_call x1, Pallas kernels, on_device(): pl.pallas_call(tail, out_shape=(shape((1, LOC), F32), shape((1, TOP), F32...  16.7 us
    pallas_call x1, Pallas kernels, on_device(): pl.pallas_call(joining, out_shape=(shape((1, T), F32), shape((5, S, T), F...  5.89 us

profile of v4, /device:TPU:1, one launch (start us, length us, event | category | flops | bytes accessed | tf_op | source)
XLA Modules:
  0.0 53.3 jit_solution(14048279306218471633)
XLA Ops:
  0.6 29.1 %prepare.1 = (f32[133,64,128]{2,1,0:T(8,128)S(1)}, bf16[64,64,256]{2,1,0:T(8,128)(2,1)S(1)}, bf16[15,64,256]{2,1,0:T(8,128)(2,1)S(1)}, f32[14,64,128]{2,1,0:T(8,...) custom-call(s32[14]{0:T(128)} %parents_h.3, ...), custom_call_target="tpu_custom_call" | custom-call | tf_op jit(solution)/shard_map/prepare/pallas_call | solution.py:502
  29.7 5.9 %joining.1 = (f32[1,128]{1,0:T(1,128)}, f32[5,64,128]{2,1,0:T(8,128)S(1)}, f32[8,128]{1,0:T(8,128)S(1)}, f32[133,64,128]{2,1,0:T(8,128)S(1)}) custom-call(s32[126]{0:T(128)} %top_parents_h.1, f32[126]{0:T(128)} %top_lengths_h.3, s32[8,128]{1,0:T(8,128)S(1)} %get-tuple-element.19.links, ...), custom_call_target="tpu_custom_call", output_to_operand_aliasing={{3}: (3, {})} | custom-call | tf_op jit(solution)/shard_map/joining/pallas_call | solution.py:540
  35.6 16.7 %tail.1 = (f32[1,14]{1,0:T(1,128)S(1)}, f32[1,126]{1,0:T(1,128)S(1)}) custom-call(s32[14]{0:T(128)} %parents_h.3, s32[1,128]{1,0:T(1,128)} %bitcast.12, f32[5,64,128]{2,1,0:T(8,128)S(1)} %get-tuple-element.23.handed, f32[8,128]{1,0:T(8,128)S(1)} %get-tuple-element.24.info, bf16[15,64,256]{2,1,0:T(8,128)(2,1)S(1)} %get-tuple-element.25.w_loc, ...), custom_call_target="tpu_custom_call" | custom-call | tf_op jit(solution)/shard_map/tail/pallas_call | solution.py:560
  52.3 0.5 copy.18
  52.8 0.5 copy.19

commit v5 on v4

--- a/solution.py
+++ b/solution.py
@@ -121,7 +121,7 @@
     for partner in partners:
         pl.semaphore_signal(barrier, inc=1, device_id=device(*partner), device_id_type=MESH)
 
-    for load in loads[:5]:
+    for load in loads[:7]:
         load.wait()
     lam_row = lam[...]
     lam_col = column(lam_row)
@@ -143,13 +143,12 @@
         result = jnp.dot(jnp.concatenate(scaled, axis=0), left_stack, preferred_element_type=F32)
         return [pack(eye2 + result[S * i:S * (i + 1)]) for i in range(len(ts))]
 
-    for c, w in enumerate(branches([lengths[c] for c in range(LOC)] + [top_lengths[me]])):
+    for c, w in enumerate(branches([lengths[c] for c in range(LEAVES)])):
         w_loc[c] = w
-
-    loads[5].wait()
-    loads[6].wait()
-    for c in range(LEAVES):
-        m_loc[c] = apply(w_loc[c], tips[c])
+        m_loc[c] = apply(w, tips[c])
+    inner = branches([lengths[c] for c in range(LEAVES, LOC)] + [top_lengths[me]])
+    for c, w in enumerate(inner):
+        w_loc[LEAVES + c] = w
     factors = []
     for n in range(LEAVES, LOC + 1):
         a, b = local_children(parents, n)
@@ -294,8 +293,8 @@
 COPIES = 3 * (NZ + 1) + 2 * (NZ - 1) + 2 * NZ
 
 
-def joining(top_parents_h, top_lengths_h, links, msg_in, w_top, freq, loglik, handed, info, msg,
-            top_parents, top_lengths, path, factor, arrs, sem):
+def joining(top_parents_h, top_lengths_h, links, msg_in, w_top, handed, info, factor, msg,
+            top_parents, top_lengths, path, arrs, sem):
     del msg_in
     loads = [pltpu.make_async_copy(src, dst, sem.at[i]) for i, (src, dst) in enumerate((
         (top_parents_h, top_parents), (top_lengths_h, top_lengths)))]
@@ -304,10 +303,6 @@
     me = lax.axis_index("leaf")
     slot = slot_of(me // (2 * NZ), lax.rem(me // 2, NZ), lax.rem(me, 2))
     factor[...] = jnp.ones((72, T), F32)
-    local_logs = msg[0, pl.ds(S - 1, 1)]
-    for g in range(1, GROUPS):
-        local_logs += msg[g, pl.ds(S - 1, 1)]
-
     def late(n):
         return links[0, n]
 
@@ -335,12 +330,6 @@
 
     lax.while_loop(lambda n: n < ROOT, climb, jnp.int32(GROUPS))
 
-    freq_col = freq[...]
-    root_u = msg[late(ROOT)] * msg[early(ROOT)]
-    likelihood = jnp.sum(freq_col * root_u, axis=0, keepdims=True)
-    row = iota((72, T), 0)
-    top_logs = -jnp.sum(jnp.log(jnp.where(row < TOP - GROUPS, factor[...], 1.0)), axis=0, keepdims=True)
-    loglik[...] = (jnp.log(likelihood) + top_logs + local_logs) * (1.0 / (GROUPS * LEAVES))
     for load in loads:
         load.wait()
 
@@ -374,6 +363,7 @@
     handed[2] = arrs[at]
     handed[3] = msg[node]
     handed[4] = msg[late(node)] * msg[early(node)] * factor[pl.ds(node - GROUPS, 1)]
+    handed[5] = msg[late(ROOT)] * msg[early(ROOT)]
     row = iota((8, T), 0)
     info[...] = jnp.where(row == 0, top_lengths[node], jnp.where(counted, node, -1).astype(F32))
 
@@ -381,7 +371,7 @@
 PHASES = ("yc", "x", "z")
 
 
-def tail(parents_h, weights_h, handed, info, w_loc, m_loc, y_loc, eig_w, inv_w, basis, lam, freq, local_out, top_out,
+def tail(parents_h, weights_h, handed, info, factor, msg, w_loc, m_loc, y_loc, eig_w, inv_w, basis, lam, freq, out,
          parents, weights, o_loc, rows, *rest):
     bufs, parts = rest[:len(PHASES)], rest[len(PHASES):2 * len(PHASES)]
     in_sem, send_sem, recv_sem = rest[2 * len(PHASES):]
@@ -445,6 +435,13 @@
     node = info[1:2]
     top_row = jnp.where(lane == me, sums[0:1, 16:17], 0.0) + jnp.where(lane.astype(F32) == node, sums[0:1, 17:18], 0.0)
     parts[0][...] = jnp.concatenate([sums[0:1], top_row], axis=0)
+
+    logs = [msg[g, pl.ds(S - 1, 1)] for g in range(GROUPS)]
+    while len(logs) > 1:
+        logs = [a + b for a, b in zip(logs[::2], logs[1::2])]
+    inner = -jnp.sum(jnp.log(jnp.where(iota((72, T), 0) < TOP - GROUPS, factor[...], 1.0)), axis=0, keepdims=True)
+    likelihood = jnp.sum(freq_col * handed[5], axis=0, keepdims=True)
+    loglik = (jnp.log(likelihood) + inner + logs[0]) * (1.0 / (GROUPS * LEAVES))
     pl.semaphore_wait(barrier, sum(map(len, offsets)))
 
     k = 0
@@ -473,16 +470,21 @@
                 local = local + buf[2 * n + here["c"], 0:1]
                 total = total + (buf[2 * n, 1:2] + buf[2 * n + 1, 1:2])
             weight_total = local[:, LOC:LOC + 1]
-            local_out[...] = (local / weight_total)[:, :LOC]
         else:
             total = buf[0]
             for n in range(1, len(some) + 1):
                 total = total + buf[n]
         if i + 1 < len(PHASES):
             parts[i + 1][...] = total
-    top_out[...] = (total / weight_total)[:, :TOP]
+    out[...] = jnp.concatenate([local / weight_total, total / weight_total, loglik], axis=0)
     for copy in copies:
         copy.wait_send()
+
+
+def finish(rows, local, top, loglik):
+    local[...] = rows[0:1, :LOC]
+    top[...] = rows[1:2, :TOP]
+    loglik[...] = rows[2:3]
 
 
 def phase_offsets(axes, sizes):
@@ -537,31 +539,30 @@
     )(*map(stay, (parents, branch_lengths, top_lengths, top_parents.reshape(1, TOP), tips, eig_vectors, eig_inverse,
                    eig_values.reshape(1, S), labeled_rates, root_freq.reshape(1, S))))
     w_top, w_loc, m_loc, y_loc, links, eig_w, inv_w, basis, lam, freq = made
-    loglik, handed, info, _ = pl.pallas_call(
+    handed, info, factor, msg = pl.pallas_call(
         joining,
-        out_shape=(shape((1, T), F32), shape((5, S, T), F32), shape((8, T), F32), shape(msg.shape, F32)),
-        in_specs=[hbm] * 2 + [smem] + [vmem] * 3,
+        out_shape=(shape((6, S, T), F32), shape((8, T), F32), shape((72, T), F32), shape(msg.shape, F32)),
+        in_specs=[hbm] * 2 + [smem] + [vmem] * 2,
         out_specs=(vmem,) * 4,
         input_output_aliases={3: 3},
         scratch_shapes=[
             pltpu.SMEM((TOP,), jnp.int32),
             pltpu.SMEM((TOP,), F32),
             pltpu.SMEM((64,), jnp.int32),
-            pltpu.VMEM((72, T), F32),
             pltpu.VMEM((GROUPS, S, T), F32),
             pltpu.SemaphoreType.DMA((2,)),
         ],
         compiler_params=pltpu.CompilerParams(vmem_limit_bytes=24 << 20),
         name="joining",
-    )(*map(stay, (top_parents, top_lengths)), links, msg, w_top, freq)
+    )(*map(stay, (top_parents, top_lengths)), links, msg, w_top)
     sizes = {"x": NX, "z": NZ, "c": 2, "y": lax.axis_size("site")}
     offsets = [phase_offsets(axes, sizes) for axes in PHASES]
     count = sum(map(len, offsets))
-    local, top = pl.pallas_call(
+    rows = pl.pallas_call(
         tail,
-        out_shape=(shape((1, LOC), F32), shape((1, TOP), F32)),
-        in_specs=[hbm] * 2 + [vmem] * 10,
-        out_specs=(vmem, vmem),
+        out_shape=shape((3, T), F32),
+        in_specs=[hbm] * 2 + [vmem] * 12,
+        out_specs=vmem,
         scratch_shapes=[
             pltpu.SMEM((LOC,), jnp.int32),
             pltpu.VMEM((1, T), jnp.int32),
@@ -575,7 +576,15 @@
         ],
         compiler_params=pltpu.CompilerParams(vmem_limit_bytes=24 << 20, collective_id=1, has_side_effects=True),
         name="tail",
-    )(*map(stay, (parents, weights.reshape(1, T))), handed, info, w_loc, m_loc, y_loc, eig_w, inv_w, basis, lam, freq)
+    )(*map(stay, (parents, weights.reshape(1, T))), handed, info, factor, msg, w_loc, m_loc, y_loc, eig_w, inv_w, basis, lam, freq)
+    local, top, loglik = pl.pallas_call(
+        finish,
+        out_shape=(shape((1, LOC), F32), shape((1, TOP), F32), shape((1, T), F32)),
+        in_specs=[vmem],
+        out_specs=(vmem,) * 3,
+        compiler_params=pltpu.CompilerParams(vmem_limit_bytes=4 << 20),
+        name="finish",
+    )(rows)
     return local.reshape(LOC), top.reshape(TOP), loglik.reshape(T)
 
 

time: 54.1 us -> 53.1 us (0.982); the launches traced: 53.3 us -> 52.9 us
  local copies, waits for them, and re-layouts: 1.02 us -> 0 us
  Pallas kernels: 51.7 us -> 52.3 us
    unnamed x2 -> x0, local copies, waits for them, and re-layouts: 1.02 us -> none
    pallas_call x2 -> x3, Pallas kernels: 22.6 us -> 23.5 us  [the longest x1 18 us: on_device(): pl.pallas_call(tail, out_shape=shape((3, T), F32), in_specs=[hbm] * 2 + [...]
where the time goes in v5:
time: 53.1 us; the launch traced here: 52.9 us
  Pallas kernels  52.3 us (98%)
  between operations  0.66 us (1%)
    pallas_call x1, Pallas kernels, on_device(): pl.pallas_call(prepare, out_shape=(shape((ROOT + 1 + WIN, S, T), F32), sh...  28.7 us
    pallas_call x1, Pallas kernels, on_device(): pl.pallas_call(tail, out_shape=shape((3, T), F32), in_specs=[hbm] * 2 + [...  18 us
    pallas_call x1, Pallas kernels, on_device(): pl.pallas_call(joining, out_shape=(shape((6, S, T), F32), shape((8, T), F...  4.97 us

profile of v5, /device:TPU:1, one launch (start us, length us, event | category | flops | bytes accessed | tf_op | source)
XLA Modules:
  0.0 52.9 jit_solution(10923949147382554887)
XLA Ops:
  0.6 28.7 %prepare.1 = (f32[133,64,128]{2,1,0:T(8,128)S(1)}, bf16[64,64,256]{2,1,0:T(8,128)(2,1)S(1)}, bf16[15,64,256]{2,1,0:T(8,128)(2,1)S(1)}, f32[14,64,128]{2,1,0:T(8,...) custom-call(s32[14]{0:T(128)} %parents_h.3, ...), custom_call_target="tpu_custom_call" | custom-call | tf_op jit(solution)/shard_map/prepare/pallas_call | solution.py:504
  29.4 5.0 %joining.1 = (f32[6,64,128]{2,1,0:T(8,128)S(1)}, f32[8,128]{1,0:T(8,128)S(1)}, f32[72,128]{1,0:T(8,128)S(1)}, f32[133,64,128]{2,1,0:T(8,128)S(1)}) custom-call(s32[126]{0:T(128)} %top_parents_h.1, f32[126]{0:T(128)} %top_lengths_h.3, s32[8,128]{1,0:T(8,128)S(1)} %get-tuple-element.21.links, ...), custom_call_target="tpu_custom_call", output_to_operand_aliasing={{3}: (3, {})} | custom-call | tf_op jit(solution)/shard_map/joining/pallas_call | solution.py:542
  34.3 18.0 %tail.1.rows = f32[3,128]{1,0:T(4,128)S(1)} custom-call(s32[14]{0:T(128)} %parents_h.3, s32[1,128]{1,0:T(1,128)} %bitcast.10, f32[6,64,128]{2,1,0:T(8,128)S(1)} %get-tuple-element.24.handed, f32[8,128]{1,0:T(8,128)S(1)} %get-tuple-element.25.info, f32[72,128]{1,0:T(8,128)S(1)} %get-tuple-element.26.factor, f32[133,64,128]{2,1,0:T(8,128)S(1)} %get-tuple-element.27.msg, ...), custom_call_target="tpu_custom_call" | custom-call | tf_op jit(solution)/shard_map/tail/pallas_call | solution.py:561
  52.4 0.5 finish.1

commit v6 on v5

--- a/solution.py
+++ b/solution.py
@@ -258,6 +258,7 @@
         crossed.append(across(dz, main))
 
     shared()
+    products(0, 5)
     for i, dz in enumerate(order):
         from_z[dz].wait_recv()
         from_x[dz] = along_x(dz, main)
@@ -270,7 +271,6 @@
             close()
         if i in (1, 3, 5):
             matrices(i - 1, i + 1)
-    products(0, 5)
     for i, dz in enumerate(order):
         groups[dz].wait_recv()
         crossed.append(across(dz, rest))
@@ -368,7 +368,7 @@
     info[...] = jnp.where(row == 0, top_lengths[node], jnp.where(counted, node, -1).astype(F32))
 
 
-PHASES = ("yc", "x", "z")
+PHASES = ("y", "cx", "z")
 
 
 def tail(parents_h, weights_h, handed, info, factor, msg, w_loc, m_loc, y_loc, eig_w, inv_w, basis, lam, freq, out,
@@ -464,11 +464,10 @@
         for arrival in arrivals:
             arrival.wait_recv()
         if i == 0:
-            local = buf[here["c"], 0:1]
-            total = buf[0, 1:2] + buf[1, 1:2]
+            local, total = buf[0, 0:1], buf[0, 1:2]
             for n in range(1, sizes["y"]):
-                local = local + buf[2 * n + here["c"], 0:1]
-                total = total + (buf[2 * n, 1:2] + buf[2 * n + 1, 1:2])
+                local = local + buf[n, 0:1]
+                total = total + buf[n, 1:2]
             weight_total = local[:, LOC:LOC + 1]
         else:
             total = buf[0]

time: 53.1 us -> 53.3 us (level)
    pallas_call x1, Pallas kernels: 4.97 us -> 5.9 us  [on_device(): pl.pallas_call(joining, out_shape=(shape((6, S, T), F32), shape((8, T), F...]
    pallas_call x1, Pallas kernels: 18 us -> 17.3 us  [on_device(): pl.pallas_call(tail, out_shape=shape((3, T), F32), in_specs=[hbm] * 2 + [...]
where the time goes in v6:
time: 53.3 us; the launch traced here: 53.1 us
  Pallas kernels  52.5 us (98%)
  between operations  0.66 us (1%)
    pallas_call x1, Pallas kernels, on_device(): pl.pallas_call(prepare, out_shape=(shape((ROOT + 1 + WIN, S, T), F32), sh...  28.7 us
    pallas_call x1, Pallas kernels, on_device(): pl.pallas_call(tail, out_shape=shape((3, T), F32), in_specs=[hbm] * 2 + [...  17.3 us
    pallas_call x1, Pallas kernels, on_device(): pl.pallas_call(joining, out_shape=(shape((6, S, T), F32), shape((8, T), F...  5.9 us

profile of v6, /device:TPU:1, one launch (start us, length us, event | category | flops | bytes accessed | tf_op | source)
XLA Modules:
  0.0 53.1 jit_solution(1395400338320128448)
XLA Ops:
  0.6 28.7 %prepare.1 = (f32[133,64,128]{2,1,0:T(8,128)S(1)}, bf16[64,64,256]{2,1,0:T(8,128)(2,1)S(1)}, bf16[15,64,256]{2,1,0:T(8,128)(2,1)S(1)}, f32[14,64,128]{2,1,0:T(8,...) custom-call(s32[14]{0:T(128)} %parents_h.3, ...), custom_call_target="tpu_custom_call" | custom-call | tf_op jit(solution)/shard_map/prepare/pallas_call | solution.py:503
  29.4 5.9 %joining.1 = (f32[6,64,128]{2,1,0:T(8,128)S(1)}, f32[8,128]{1,0:T(8,128)S(1)}, f32[72,128]{1,0:T(8,128)S(1)}, f32[133,64,128]{2,1,0:T(8,128)S(1)}) custom-call(s32[126]{0:T(128)} %top_parents_h.1, f32[126]{0:T(128)} %top_lengths_h.3, s32[8,128]{1,0:T(8,128)S(1)} %get-tuple-element.21.links, ...), custom_call_target="tpu_custom_call", output_to_operand_aliasing={{3}: (3, {})} | custom-call | tf_op jit(solution)/shard_map/joining/pallas_call | solution.py:541
  35.3 17.3 %tail.1.rows = f32[3,128]{1,0:T(4,128)S(1)} custom-call(s32[14]{0:T(128)} %parents_h.3, s32[1,128]{1,0:T(1,128)} %bitcast.10, f32[6,64,128]{2,1,0:T(8,128)S(1)} %get-tuple-element.24.handed, f32[8,128]{1,0:T(8,128)S(1)} %get-tuple-element.25.info, f32[72,128]{1,0:T(8,128)S(1)} %get-tuple-element.26.factor, f32[133,64,128]{2,1,0:T(8,128)S(1)} %get-tuple-element.27.msg, ...), custom_call_target="tpu_custom_call" | custom-call | tf_op jit(solution)/shard_map/tail/pallas_call | solution.py:560
  52.6 0.5 finish.1

commit v7 on v5

--- a/solution.py
+++ b/solution.py
@@ -16,6 +16,8 @@
 TOP = 126
 ROOT = 126
 WIN = 6
+NARROW = 3
+TURN = 102
 ACROSS = 16
 F32 = jnp.float32
 BF16 = jnp.bfloat16
@@ -309,11 +311,11 @@
     def early(n):
         return links[1, n]
 
-    def climb(n):
+    def climb(width, n):
         done = []
         fits = True
         steps = jnp.int32(1)
-        for j in range(WIN):
+        for j in range(width):
             k = jnp.minimum(n + j, T - 1) if j > 1 else n + j
             a, b = late(k), early(k)
             if j:
@@ -328,7 +330,8 @@
             factor[pl.ds(n + j - GROUPS, 1)] = r
         return n + steps
 
-    lax.while_loop(lambda n: n < ROOT, climb, jnp.int32(GROUPS))
+    reached = lax.while_loop(lambda n: n < TURN, functools.partial(climb, WIN), jnp.int32(GROUPS))
+    lax.while_loop(lambda n: n < ROOT, functools.partial(climb, NARROW), reached)
 
     for load in loads:
         load.wait()

time: 53.1 us -> 53.3 us (level)
    pallas_call x1, Pallas kernels: 4.97 us -> 6.31 us  [on_device(): pl.pallas_call(joining, out_shape=(shape((6, S, T), F32), shape((8, T), F...]
    pallas_call x1, Pallas kernels: 18 us -> 17 us  [on_device(): pl.pallas_call(tail, out_shape=shape((3, T), F32), in_specs=[hbm] * 2 + [...]
where the time goes in v7:
time: 53.3 us; the launch traced here: 53.2 us
  Pallas kernels  52.6 us (99%)
  between operations  0.66 us (1%)
    pallas_call x1, Pallas kernels, on_device(): pl.pallas_call(prepare, out_shape=(shape((ROOT + 1 + WIN, S, T), F32), sh...  28.7 us
    pallas_call x1, Pallas kernels, on_device(): pl.pallas_call(tail, out_shape=shape((3, T), F32), in_specs=[hbm] * 2 + [...  17 us
    pallas_call x1, Pallas kernels, on_device(): pl.pallas_call(joining, out_shape=(shape((6, S, T), F32), shape((8, T), F...  6.31 us

profile of v7, /device:TPU:1, one launch (start us, length us, event | category | flops | bytes accessed | tf_op | source)
XLA Modules:
  0.0 53.2 jit_solution(6276730577689610751)
XLA Ops:
  0.6 28.7 %prepare.1 = (f32[133,64,128]{2,1,0:T(8,128)S(1)}, bf16[64,64,256]{2,1,0:T(8,128)(2,1)S(1)}, bf16[15,64,256]{2,1,0:T(8,128)(2,1)S(1)}, f32[14,64,128]{2,1,0:T(8,...) custom-call(s32[14]{0:T(128)} %parents_h.3, ...), custom_call_target="tpu_custom_call" | custom-call | tf_op jit(solution)/shard_map/prepare/pallas_call | solution.py:507
  29.4 6.3 %joining.1 = (f32[6,64,128]{2,1,0:T(8,128)S(1)}, f32[8,128]{1,0:T(8,128)S(1)}, f32[72,128]{1,0:T(8,128)S(1)}, f32[133,64,128]{2,1,0:T(8,128)S(1)}) custom-call(s32[126]{0:T(128)} %top_parents_h.1, f32[126]{0:T(128)} %top_lengths_h.3, s32[8,128]{1,0:T(8,128)S(1)} %get-tuple-element.21.links, ...), custom_call_target="tpu_custom_call", output_to_operand_aliasing={{3}: (3, {})} | custom-call | tf_op jit(solution)/shard_map/joining/pallas_call | solution.py:545
  35.7 17.0 %tail.1.rows = f32[3,128]{1,0:T(4,128)S(1)} custom-call(s32[14]{0:T(128)} %parents_h.3, s32[1,128]{1,0:T(1,128)} %bitcast.10, f32[6,64,128]{2,1,0:T(8,128)S(1)} %get-tuple-element.24.handed, f32[8,128]{1,0:T(8,128)S(1)} %get-tuple-element.25.info, f32[72,128]{1,0:T(8,128)S(1)} %get-tuple-element.26.factor, f32[133,64,128]{2,1,0:T(8,128)S(1)} %get-tuple-element.27.msg, ...), custom_call_target="tpu_custom_call" | custom-call | tf_op jit(solution)/shard_map/tail/pallas_call | solution.py:564
  52.7 0.5 finish.1
